TPU v7x, 32 devices: a whole 2x2x4 slice. The times are simulated.
32 devices in a mesh: rcv: 8 (over z, y), src: 4 (over x, core).
Axes of the slice: x: 2, y: 2, z: 4, core: 2. Of those that a mesh axis runs over, the one named last changes fastest.
Arguments:
- rb_data: float32 [32, 64, 512], P('rcv', 'src'), may hold values from -6 to 6
- bs_data: float32 [64, 64, 512], P('rcv', 'src'), may hold values from -0.046875 to 0.046875
- recorded: float32 [32, 64, 512], P('rcv', 'src'), may hold values from -6 to 6
- filters: float32 [3, 21, 32, 64], P(None, None, 'rcv', 'src'), may hold values from -0.9 to 0.9
- offsets: int32 [21], replicated, may hold values from -20 to 20, as said below
Outputs:
- primaries: float32 [32, 64, 512], P('rcv', 'src')
Inputs may be any that keep to these rules, and one draw needn't show every extreme that they name: The 21 offsets are distinct, and both -20 and 20 are among them.
All inputs are finite; a program needn't handle non-finite values.
Results may differ from a plain program's by a relative error of at most 0.000073.
Values sent between devices are 32-bit elements; how exact they have to be, the bound alone decides.
No kernel may reach another device: no remote copies, remote signals or barrier semaphores. Data moves between devices by JAX's collectives and lax.ppermute only.
A program may use at most 64 MiB of HBM per device.

v0:
```python
import functools
import math

import jax
import jax.numpy as jnp
import numpy as np
from jax import lax
from jax.experimental import pallas as pl
from jax.experimental.pallas import tpu as pltpu
from jax.sharding import PartitionSpec as P

LANES = 128
SUBLANES = 8
VMEM_LIMIT = 40 * 1024 * 1024
AXES = ("rcv", "src")
STEP = 32
GROUP = 4
CHUNK = 64


def phases(samples):
    fine = np.arange(STEP, dtype=np.int64)
    coarse = np.arange(0, samples, STEP, dtype=np.int64)
    times = np.concatenate([coarse, fine])[:, None]
    odd = 2 * np.arange(samples, dtype=np.int64)[None, :] + 1
    phase = (times * odd % (4 * samples)).astype(np.float64) * (math.pi / (2 * samples))
    return np.concatenate([np.cos(phase), np.sin(phase)], axis=0).astype(np.float32)


def dft_tables(high_ref, low_ref, phases_ref):
    samples = high_ref.shape[0]
    coarse = samples // STEP
    half = phases_ref.shape[0] // 2
    cos_fine = phases_ref[coarse:half]
    sin_fine = phases_ref[half + coarse :]
    for step in range(coarse):
        cos_step = phases_ref[step : step + 1]
        sin_step = phases_ref[half + step : half + step + 1]
        cosine = cos_step * cos_fine - sin_step * sin_fine
        sine = sin_step * cos_fine + cos_step * sin_fine
        for value, at in ((cosine, 0), (-sine, samples)):
            high = value.astype(jnp.bfloat16)
            where = (pl.ds(step * STEP, STEP), pl.ds(at, samples))
            high_ref[where] = high
            low_ref[where] = (value - high.astype(jnp.float32)).astype(jnp.bfloat16)


def split_dot(rows, high_table, low_table, of=0):
    high = rows.astype(jnp.bfloat16)
    low = (rows - high.astype(jnp.float32)).astype(jnp.bfloat16)

    def dot(left, right):
        return lax.dot_general(
            left, right, (((1,), (of,)), ((), ())), preferred_element_type=jnp.float32
        )

    return dot(high, high_table) + (dot(low, high_table) + dot(high, low_table))


def spectra(traces_ref, tables):
    lead = traces_ref.shape[:-1]
    samples = traces_ref.shape[-1]
    rows = math.prod(lead)
    return split_dot(traces_ref[...].reshape(rows, samples), *tables).reshape(lead + (2 * samples,))


def with_sums(values):
    half = values.shape[-1] // 2
    total = values[..., :half] + values[..., half:]
    return jnp.concatenate([values, total], axis=-1)


def products(total_ref, lefts, right_ref):
    _, sources, width = total_ref.shape
    half = width // 2
    zero = jnp.zeros((sources, LANES), jnp.float32)
    for tile in range(half // LANES):
        real = pl.ds(tile * LANES, LANES)
        imag = pl.ds(half + tile * LANES, LANES)
        both = pl.ds(width + tile * LANES, LANES)
        for group in range(0, len(lefts), GROUP):
            members = lefts[group : group + GROUP]
            sums = [(zero, zero, zero) for _ in members]
            for bounce in range(right_ref.shape[0]):
                at = slice(bounce, bounce + 1)
                right_real = right_ref[bounce, :, real]
                right_imag = right_ref[bounce, :, imag]
                right_more = right_imag - right_real
                right_both = right_imag + right_real
                for index, (_, left_ref, row) in enumerate(members):
                    one, two, three = sums[index]
                    sums[index] = (
                        one + left_ref[row, at, both] * right_real,
                        two + left_ref[row, at, real] * right_more,
                        three + left_ref[row, at, imag] * right_both,
                    )
            for (one, two, three), (row, _, _) in zip(sums, members):
                total_ref[row, :, real] = one - three
                total_ref[row, :, imag] = one + two


def to_traces(prediction_ref, total_ref, tables):
    rows, sources, width = total_ref.shape
    flat = total_ref[...].reshape(rows * sources, width) * (2.0 / width)
    prediction_ref[...] = split_dot(flat, *tables, of=1).reshape(prediction_ref.shape)


def lay_weights(weights_ref, scratch, filters_ref):
    near, receivers, sources, taps = filters_ref.shape
    scratch[...] = jnp.zeros(scratch.shape, jnp.float32)
    lanes = receivers * sources
    for copy in range(LANES // lanes):
        for step in range(near):
            for receiver in range(receivers):
                rows = pl.ds(copy * lanes + receiver * sources, sources)
                scratch[rows, step * taps : (step + 1) * taps] = filters_ref[step, receiver]
    weights_ref[...] = scratch[...].T[: weights_ref.shape[0]]


def matched(prediction_ref, weights_ref, offsets_ref, turned, sums):
    extended, sources, samples = prediction_ref.shape
    taps = offsets_ref.shape[0]
    receivers = extended - 2
    lanes = receivers * sources
    parts = LANES // lanes
    per = samples // parts
    zero = jnp.zeros((lanes, LANES), jnp.float32)
    for near in range(3):
        for block in range(per // LANES + 2):
            side = []
            for part in range(parts):
                at = part * per + (block - 1) * LANES
                if 0 <= at < samples:
                    rows = prediction_ref[pl.ds(near, receivers), :, at : at + LANES]
                    side.append(rows.reshape(lanes, LANES))
                else:
                    side.append(zero)
            turned[near, pl.ds(block * LANES, LANES)] = jnp.concatenate(side, axis=0).T
    chunk = min(per, CHUNK)
    for first in range(0, per, chunk):
        total = jnp.zeros((chunk, LANES), jnp.float32)
        for tap in range(taps):
            start = LANES + first - offsets_ref[tap]
            for near in range(3):
                at = near * taps + tap
                total = total + weights_ref[at : at + 1] * turned[near, pl.ds(start, chunk), :]
        sums[pl.ds(first, chunk)] = total
    back = jnp.concatenate(
        [sums[at : at + LANES].T for at in range(0, per, LANES)], axis=1
    ).reshape(parts, receivers, sources, per)
    return jnp.concatenate([back[part] for part in range(parts)], axis=2)


def first_kernel(phases_ref, here_ref, right_ref, high_ref, low_ref, here_out, right_out):
    dft_tables(high_ref, low_ref, phases_ref)
    tables = (high_ref[...], low_ref[...])
    here_out[...] = with_sums(spectra(here_ref, tables))
    right_out[...] = spectra(right_ref, tables)


def second_kernel(high_ref, low_ref, filters_ref, one_ref, *refs):
    right_refs, (weights_ref, one_out, right_out, turned) = refs[:-4], refs[-4:]
    lay_weights(weights_ref, turned, filters_ref)
    tables = (high_ref[...], low_ref[...])
    one_out[...] = with_sums(spectra(one_ref, tables))
    held = right_refs[0].shape[0]
    for block, ref in enumerate(right_refs):
        right_out[pl.ds(block * held, held)] = spectra(ref, tables)


def place_of(column, slot, slots, held):
    first = jnp.bitwise_xor(column, slot) % slots * held
    return pl.ds(pl.multiple_of(first, held), held)


def edge_kernel(slots, where_ref, *refs):
    near_ref, far_ref = refs[3 * slots :]
    odd, column, same = where_ref[0] % 2 == 1, where_ref[1], where_ref[2] == 1
    receivers, held, _ = refs[0].shape
    for slot in range(slots):
        these = place_of(column, slot, slots, held)
        here, one, two = refs[3 * slot : 3 * slot + 3]
        for index, (yes, no) in enumerate(((here, one), (one, two))):
            first = jnp.where(same, yes[0], no[0])
            last = jnp.where(same, yes[receivers - 1], no[receivers - 1])
            near_ref[index, these] = jnp.where(odd, first, last)
            far_ref[index, these] = jnp.where(odd, last, first)


def main_kernel(
    slots, blocks, where_ref, high_ref, low_ref, right_a, right_b, here_ref, one_ref, *refs
):
    columns, refs = refs[: 3 * slots - 2], refs[3 * slots - 2 :]
    right_refs, (total_ref, right_ref, own_ref, left_ref) = refs[:-4], refs[-4:]
    tables = (high_ref[...], low_ref[...])
    row, column, same = where_ref[0], where_ref[1], where_ref[2] == 1
    count = right_a.shape[0]
    block = 0
    for ref, done in ((right_a, True), (right_b, True)) + tuple((r, False) for r in right_refs):
        for first in range(0, ref.shape[0], count):
            value = ref[pl.ds(first, count)] if done else spectra(ref, tables)
            at = jnp.bitwise_xor(row, block) % blocks * count
            right_ref[pl.ds(at, count)] = value
            block += 1
    receivers, held, _ = here_ref.shape
    for slot in range(slots):
        these = place_of(column, slot, slots, held)
        if slot == 0:
            two = with_sums(spectra(columns[0], tables))
            own = jnp.where(same, here_ref[...], one_ref[...])
            mirror = jnp.where(same, one_ref[...], two)
        else:
            here, one, two = [ref[...] for ref in columns[3 * slot - 2 : 3 * slot + 1]]
            chosen = jnp.concatenate([jnp.where(same, here, one), jnp.where(same, one, two)])
            flat = chosen.reshape(2 * receivers * held, chosen.shape[-1])
            value = with_sums(split_dot(flat, *tables)).reshape(2 * receivers, held, -1)
            own, mirror = value[:receivers], value[receivers:]
        for receiver in range(receivers):
            own_ref[receiver, these] = own[receiver]
            left_ref[receiver, these] = mirror[receiver]
    products(total_ref, [(row, left_ref, row) for row in range(receivers)], right_ref)


def mirror_kernel(
    blocks, where_ref, offsets_ref, high_ref, low_ref, weights_ref, near_ref, far_ref,
    start_ref, right_ref, out_ref, halo_ref, total, prediction, turned, sums, outer,
):
    receivers = out_ref.shape[0]
    row = where_ref[0]
    odd, lower = row % 2 == 1, row < blocks
    before = jnp.where(odd, near_ref[...], far_ref[...])
    after = jnp.where(odd, far_ref[...], near_ref[...])
    zero = jnp.zeros(before.shape[1:], jnp.float32)
    for which, (value, end, none) in enumerate(
        (
            (before, row % blocks == 0, lower),
            (after, row % blocks == blocks - 1, jnp.logical_not(lower)),
        )
    ):
        own, mirror = value[0], value[1]
        outer[which] = jnp.where(end, jnp.where(none, zero, mirror), own)
        outer[2 + which] = jnp.where(end, jnp.where(none, own, zero), mirror)
    tables = (high_ref[...], low_ref[...])
    halo_ref[...] = with_sums(spectra(outer, tables))
    total[pl.ds(1, receivers)] = start_ref[...]
    products(total, [(0, halo_ref, 2), (receivers + 1, halo_ref, 3)], right_ref)
    to_traces(prediction, total, tables)
    out_ref[...] = matched(prediction, weights_ref, offsets_ref, turned, sums)


def own_kernel(
    offsets_ref, high_ref, low_ref, weights_ref, right_ref, left_ref, halo_ref, recorded_ref,
    out_ref, total, prediction, turned, sums,
):
    receivers = out_ref.shape[0]
    lefts = [(1 + row, left_ref, row) for row in range(receivers)]
    products(total, [(0, halo_ref, 0)] + lefts + [(receivers + 1, halo_ref, 1)], right_ref)
    to_traces(prediction, total, (high_ref[...], low_ref[...]))
    out_ref[...] = recorded_ref[...] - matched(
        prediction, weights_ref, offsets_ref, turned, sums
    )


def last_kernel(part_ref, arrived_ref, out_ref):
    out_ref[...] = part_ref[...] - arrived_ref[...]


def call(kernel, scalars, arrays, outs, scratch, in_hbm=0):
    shapes = [s if hasattr(s, "dtype") else jax.ShapeDtypeStruct(s, jnp.float32) for s in outs]
    vmem = pl.BlockSpec(memory_space=pltpu.VMEM)
    return pl.pallas_call(
        kernel,
        out_shape=shapes,
        in_specs=[pl.BlockSpec(memory_space=pltpu.SMEM)] * len(scalars)
        + [pl.BlockSpec(memory_space=pltpu.HBM)] * in_hbm
        + [vmem] * (len(arrays) - in_hbm),
        out_specs=[vmem] * len(shapes),
        scratch_shapes=[
            s if not isinstance(s, tuple) else pltpu.VMEM(s, jnp.float32) for s in scratch
        ],
        compiler_params=pltpu.CompilerParams(vmem_limit_bytes=VMEM_LIMIT),
    )(*scalars, *arrays)


def local(rows, columns, rb_data, bs_data, recorded, filters, offsets):
    receivers, left_count, samples = rb_data.shape
    right_count, sources, _ = bs_data.shape
    taps = offsets.shape[0]
    slots, blocks = columns // 2, rows // 2
    row, column = lax.axis_index("rcv"), lax.axis_index("src")
    same = row // blocks == column // slots
    where = jnp.stack([row, column, same]).astype(jnp.int32)

    def permute(array, target):
        pairs = []
        for i in range(rows):
            for j in range(columns):
                to = target(i, j)
                if to is not None and 0 <= to[0] < rows:
                    pairs.append((i * columns + j, to[0] * columns + to[1]))
        return lax.ppermute(array, AXES, pairs)

    def is_same(i, j):
        return i // blocks == j // slots

    def other_rows(first, end):
        return [permute(bs_data, lambda i, j, k=k: (i ^ k, j)) for k in range(first, end)]

    cut = 2 * blocks // 3 + 1
    width = 2 * samples
    held = slots * left_count
    one = permute(
        rb_data, lambda i, j: (i, j ^ slots) if is_same(i, j) else (i ^ blocks, j)
    )
    some = other_rows(1, cut)
    heres = [rb_data] + [
        permute(rb_data, lambda i, j, k=k: (i, j ^ k)) for k in range(1, slots)
    ]
    table = jax.ShapeDtypeStruct((samples, width), jnp.bfloat16)
    left_shape = (receivers, left_count, width + samples)
    high, low, here_spectra, right_a = call(
        first_kernel, [], [jnp.asarray(phases(samples)), rb_data, bs_data],
        [table, table, left_shape, (right_count, sources, width)], [],
    )
    one, some, heres, high, low, here_spectra, right_a = lax.optimization_barrier(
        (one, some, heres, high, low, here_spectra, right_a)
    )
    gathered = []
    for k in range(slots):
        if k > 0:
            gathered.append(heres[k])
            gathered.append(permute(one, lambda i, j, k=k: (i, j ^ k)))
        gathered.append(
            permute(one, lambda i, j, k=k: (i, j ^ slots ^ k) if is_same(i, j) else None)
        )
    rest = other_rows(cut, blocks)
    weights, one_spectra, right_b = call(
        second_kernel, [], [high, low, filters.transpose(0, 2, 3, 1), one] + some,
        [
            (-(-3 * taps // SUBLANES) * SUBLANES, LANES),
            left_shape,
            (len(some) * right_count, sources, width),
        ],
        [(LANES, LANES)],
    )
    gathered, rest, weights, one_spectra, right_b = lax.optimization_barrier(
        (gathered, rest, weights, one_spectra, right_b)
    )
    edge_shape = (2, held, samples)
    near, far = call(
        functools.partial(edge_kernel, slots), [where], [rb_data, one] + gathered,
        [edge_shape, edge_shape], [],
    )

    def in_half(i, at):
        return at % blocks + i // blocks * blocks

    near = permute(near, lambda i, j: (i ^ 1, j))
    far = permute(far, lambda i, j: (in_half(i, i + 1 if i % 2 else i - 1), j))
    mirror_weights = permute(weights, lambda i, j: (i ^ blocks, j))
    per = samples * receivers * sources // LANES
    total, right, own_left = call(
        functools.partial(main_kernel, slots, blocks),
        [where],
        [high, low, right_a, right_b, here_spectra, one_spectra] + gathered + rest,
        [
            (receivers, sources, width),
            (blocks * right_count, sources, width),
            (receivers, held, width + samples),
        ],
        [(receivers, held, width + samples)],
    )
    scratch = [
        (receivers + 2, sources, width),
        (receivers + 2, sources, samples),
        (filters.shape[0], per + 2 * LANES, LANES),
        (per, LANES),
    ]
    mirror_part, halo = call(
        functools.partial(mirror_kernel, blocks),
        [where, offsets],
        [high, low, mirror_weights, near, far, total, right],
        [recorded.shape, (4, held, width + samples)],
        scratch + [(4, held, samples)],
    )
    arrived = permute(mirror_part, lambda i, j: (i ^ blocks, j))
    (own_part,) = call(
        own_kernel, [offsets], [high, low, weights, right, own_left, halo, recorded],
        [recorded.shape], scratch,
    )
    (out,) = call(last_kernel, [], [own_part, arrived], [recorded.shape], [])
    return out


def solution(mesh):
    in_specs = (
        P("rcv", "src", None),
        P("rcv", "src", None),
        P("rcv", "src", None),
        P(None, None, "rcv", "src"),
        P(),
    )
    out_specs = P("rcv", "src", None)
    body = functools.partial(local, mesh.shape["rcv"], mesh.shape["src"])
    return jax.shard_map(body, mesh=mesh, in_specs=in_specs, out_specs=out_specs, check_vma=False)
```

profile of v0, /device:TPU:0, one launch (start us, length us, event | category | flops | bytes accessed | tf_op | source)
XLA Modules:
  0.0 48.1 jit_solution(12338451197326374686)
XLA Ops:
  0.0 3.0 %collective-permute-start.1 = (f32[8,16,512]{2,1,0:T(8,128)}, f32[8,16,512]{2,1,0:T(8,128)S(1)}, u32[]{:S(2)}, u32[]{:S(2)}) collective-permute-start(f32[8,16,512]{2,1,0:T(8,128)} %right_ref.1), channel_id=1, source_target_pairs={{0,4},{1,5},{2,6},{3,7},{4,0},{5,1},{6,2},{7,3},{8,12},{9,13},{10,... | collective-permute-start | bytes 786440 | tf_op jit(solution)/shard_map/ppermute | solution.py:301
  3.0 1.6 %collective-permute-start.2 = (f32[8,16,512]{2,1,0:T(8,128)}, f32[8,16,512]{2,1,0:T(8,128)S(1)}, u32[]{:S(2)}, u32[]{:S(2)}) collective-permute-start(f32[8,16,512]{2,1,0:T(8,128)} %right_ref.1), channel_id=1, source_target_pairs={{0,8},{1,9},{2,10},{3,11},{4,12},{5,13},{6,14},{7,15},{8,0},{9,1},... | collective-permute-start | bytes 786440 | tf_op jit(solution)/shard_map/ppermute | solution.py:301
  4.5 1.5 %collective-permute-start = (f32[4,16,512]{2,1,0:T(8,128)}, f32[4,16,512]{2,1,0:T(8,128)S(1)}, u32[]{:S(2)}, u32[]{:S(2)}) collective-permute-start(f32[4,16,512]{2,1,0:T(8,128)} %refs_0_.1), channel_id=1, source_target_pairs={{0,2},{1,3},{2,18},{3,19},{4,6},{5,7},{6,22},{7,23},{8,10},{9,11},... | collective-permute-start | bytes 393224 | tf_op jit(solution)/shard_map/ppermute | solution.py:301
  6.4 0.9 %copy-done = f32[4,16,512]{2,1,0:T(8,128)S(1)} copy-done((f32[4,16,512]{2,1,0:T(8,128)S(1)}, f32[4,16,512]{2,1,0:T(8,128)}, u32[]{:S(2)}) %copy-start) | copy-done | bytes 131096
  7.3 0.9 %copy-done.4 = f32[8,16,512]{2,1,0:T(8,128)S(1)} copy-done((f32[8,16,512]{2,1,0:T(8,128)S(1)}, f32[8,16,512]{2,1,0:T(8,128)}, u32[]{:S(2)}) %copy-start.4) | copy-done | bytes 262168
  8.3 0.9 %copy-done.9 = f32[96,512]{1,0:T(8,128)S(1)} copy-done((f32[96,512]{1,0:T(8,128)S(1)}, f32[96,512]{1,0:T(8,128)}, u32[]{:S(2)}) %copy-start.9) | copy-done | bytes 196632
  9.2 1.5 %shard_map.64 = (bf16[512,1024]{1,0:T(8,128)(2,1)S(1)}, bf16[512,1024]{1,0:T(8,128)(2,1)S(1)}, f32[4,16,1536]{2,1,0:T(8,128)S(1)}, f32[8,16,1024]{2,1,0:T(8,128)S(1)}) custom-call(f32[96,512]{1,0:T(8,128)S(1)} %copy-done.9, f32[4,16,512]{2,1,0:T(8,128)S(1)} %copy-done, f32[8,16,512]{2,1,0:T(8,128)S(1)} %copy-done.4), custom_call_target="tpu_custom_call" | custom-call | tf_op jit(solution)/shard_map/pallas_call | solution.py:271
  10.8 0.7 %copy-done.2 = f32[4,16,1536]{2,1,0:T(8,128)} copy-done((f32[4,16,1536]{2,1,0:T(8,128)}, f32[4,16,1536]{2,1,0:T(8,128)S(1)}, u32[]{:S(2)}) %copy-start.2) | copy-done | bytes 393240
  11.5 0.7 %copy-done.5 = f32[8,16,512]{2,1,0:T(8,128)} copy-done((f32[8,16,512]{2,1,0:T(8,128)}, f32[8,16,512]{2,1,0:T(8,128)S(1)}, u32[]{:S(2)}) %copy-start.5) | copy-done | bytes 262168
  12.2 3.0 %collective-permute-done.2.refs_1_ = f32[8,16,512]{2,1,0:T(8,128)S(1)} collective-permute-done((f32[8,16,512]{2,1,0:T(8,128)}, f32[8,16,512]{2,1,0:T(8,128)S(1)}, u32[]{:S(2)}, u32[]{:S(2)}) %collective-permute-start.2) | collective-permute-done | bytes 262176 | tf_op jit(solution)/shard_map/ppermute | solution.py:301
  15.2 0.7 %copy-done.7 = f32[8,16,512]{2,1,0:T(8,128)} copy-done((f32[8,16,512]{2,1,0:T(8,128)}, f32[8,16,512]{2,1,0:T(8,128)S(1)}, u32[]{:S(2)}) %copy-start.7) | copy-done | bytes 262168
  15.9 3.3 %collective-permute-start.4 = (f32[4,16,512]{2,1,0:T(8,128)S(1)}, f32[4,16,512]{2,1,0:T(8,128)S(1)}, u32[]{:S(2)}, u32[]{:S(2)}) collective-permute-start(f32[4,16,512]{2,1,0:T(8,128)S(1)} %collective-permute-done.one_ref.refs_1_), channel_id=1, source_target_pairs={{0,2},{1,3},{4,6},{5,7},{8,10},{9,11},{12,14},{13,15},{18,16},{19,... | collective-permute-start | bytes 393224 | tf_op jit(solution)/shard_map/ppermute | solution.py:301
  19.3 1.4 %collective-permute-start.6 = (f32[4,16,512]{2,1,0:T(8,128)S(1)}, f32[4,16,512]{2,1,0:T(8,128)S(1)}, u32[]{:S(2)}, u32[]{:S(2)}) collective-permute-start(f32[4,16,512]{2,1,0:T(8,128)S(1)} %collective-permute-done.one_ref.refs_1_), channel_id=1, source_target_pairs={{0,3},{1,2},{4,7},{5,6},{8,11},{9,10},{12,15},{13,14},{18,17},{19,... | collective-permute-start | bytes 393224 | tf_op jit(solution)/shard_map/ppermute | solution.py:301
  20.8 1.0 %copy-done.6 = f32[8,16,512]{2,1,0:T(8,128)S(1)} copy-done((f32[8,16,512]{2,1,0:T(8,128)S(1)}, f32[8,16,512]{2,1,0:T(8,128)}, u32[]{:S(2)}) %copy-start.6) | copy-done | bytes 262168
  21.8 0.9 %copy-done.8 = f32[8,16,512]{2,1,0:T(8,128)S(1)} copy-done((f32[8,16,512]{2,1,0:T(8,128)S(1)}, f32[8,16,512]{2,1,0:T(8,128)}, u32[]{:S(2)}) %copy-start.8) | copy-done | bytes 262168
  22.7 0.9 %copy-done.11 = f32[3,21,4,16]{1,3,2,0:T(8,128)S(1)} copy-done((f32[3,21,4,16]{1,3,2,0:T(8,128)S(1)}, f32[3,21,4,16]{1,3,2,0:T(8,128)}, u32[]{:S(2)}) %copy-start.11) | copy-done | bytes 16152
  23.6 1.6 %shard_map.65 = (f32[64,128]{1,0:T(8,128)S(1)}, f32[4,16,1536]{2,1,0:T(8,128)S(1)}, f32[16,16,1024]{2,1,0:T(8,128)S(1)}) custom-call(bf16[512,1024]{1,0:T(8,128)(2,1)S(1)} %get-tuple-element.39.high_ref, bf16[512,1024]{1,0:T(8,128)(2,1)S(1)} %get-tuple-element.40.low_ref, f32[3,4,16,21]{3,2,1,0:T(8,128)S(1)} %bitcast.4, ...), custom_call_target="tpu_custom_call" | custom-call | tf_op jit(solution)/shard_map/pallas_call | solution.py:271
  26.4 2.2 %collective-permute-start.10 = (f32[2,32,512]{2,1,0:T(8,128)S(1)}, f32[2,32,512]{2,1,0:T(8,128)S(1)}, u32[]{:S(2)}, u32[]{:S(2)}) collective-permute-start(f32[2,32,512]{2,1,0:T(8,128)S(1)} %get-tuple-element.61), channel_id=1, source_target_pairs={{0,12},{1,13},{2,14},{3,15},{4,8},{5,9},{6,10},{7,11},{8,4},{9,5},... | collective-permute-start | bytes 393224 | tf_op jit(solution)/shard_map/ppermute | solution.py:301
  28.5 1.9 %collective-permute-start.8 = (f32[64,128]{1,0:T(8,128)S(1)}, f32[64,128]{1,0:T(8,128)S(1)}, u32[]{:S(2)}, u32[]{:S(2)}) collective-permute-start(f32[64,128]{1,0:T(8,128)S(1)} %get-tuple-element.48.weights_ref), channel_id=1, source_target_pairs={{0,16},{1,17},{2,18},{3,19},{4,20},{5,21},{6,22},{7,23},{8,24},{9,... | collective-permute-start | bytes 98312 | tf_op jit(solution)/shard_map/ppermute | solution.py:301
  30.4 4.0 %shard_map.66 = (f32[4,16,1024]{2,1,0:T(8,128)S(1)}, f32[32,16,1024]{2,1,0:T(8,128)S(1)}, f32[4,32,1536]{2,1,0:T(8,128)S(1)}) custom-call(s32[3]{0:T(128)S(1)} %pad_add_fusion.where_ref, bf16[512,1024]{1,0:T(8,128)(2,1)S(1)} %get-tuple-element.39.high_ref, bf16[512,1024]{1,0:T(8,128)(2,1)S(1)} %get-tuple-element.40.low_ref, ...), custom_call_target="tpu_custom_call" | custom-call | tf_op jit(solution)/shard_map/pallas_call | solution.py:271
  34.5 4.1 %shard_map.68 = (f32[4,16,512]{2,1,0:T(8,128)S(1)}, f32[4,32,1536]{2,1,0:T(8,128)S(1)}) custom-call(s32[3]{0:T(128)S(1)} %pad_add_fusion.where_ref, s32[21]{0:T(128)S(1)} %copy-done.12, bf16[512,1024]{1,0:T(8,128)(2,1)S(1)} %get-tuple-element.39.high_ref, bf16[512,1024]{1,0:T(8,128)(2,1)S(1)} %get-tuple-element.40.low_ref, ...), custom_call_target="tpu_custom_call" | custom-call | tf_op jit(solution)/shard_map/pallas_call | solution.py:271
  38.6 1.9 %collective-permute-start.11 = (f32[4,16,512]{2,1,0:T(8,128)S(1)}, f32[4,16,512]{2,1,0:T(8,128)S(1)}, u32[]{:S(2)}, u32[]{:S(2)}) collective-permute-start(f32[4,16,512]{2,1,0:T(8,128)S(1)} %get-tuple-element.64), channel_id=1, source_target_pairs={{0,16},{1,17},{2,18},{3,19},{4,20},{5,21},{6,22},{7,23},{8,24},{9,... | collective-permute-start | bytes 393224 | tf_op jit(solution)/shard_map/ppermute | solution.py:301
  40.6 5.2 %shard_map.69.part_ref = f32[4,16,512]{2,1,0:T(8,128)S(1)} custom-call(s32[21]{0:T(128)S(1)} %copy-done.12, bf16[512,1024]{1,0:T(8,128)(2,1)S(1)} %get-tuple-element.39.high_ref, bf16[512,1024]{1,0:T(8,128)(2,1)S(1)} %get-tuple-element.40.low_ref, f32[64,128]{1,0:T(8,128)S(1)} %get-tuple-element.48.weights_ref, ...), custom_call_target="tpu_custom_call" | custom-call | tf_op jit(solution)/shard_map/pallas_call | solution.py:271
  45.8 1.7 %collective-permute-done.11.arrived_ref = f32[4,16,512]{2,1,0:T(8,128)S(1)} collective-permute-done((f32[4,16,512]{2,1,0:T(8,128)S(1)}, f32[4,16,512]{2,1,0:T(8,128)S(1)}, u32[]{:S(2)}, u32[]{:S(2)}) %collective-permute-start.11) | collective-permute-done | bytes 131104 | tf_op jit(solution)/shard_map/ppermute | solution.py:301
  (34 shorter events, 2.5 us)
Async XLA Ops:
  0.0 11.5 %collective-permute-start.1 = (f32[8,16,512]{2,1,0:T(8,128)}, f32[8,16,512]{2,1,0:T(8,128)S(1)}, u32[]{:S(2)}, u32[]{:S(2)}) collective-permute-start(f32[8,16,512]{2,1,0:T(8,128)} %right_ref.1), channel_id=1, source_target_pairs={{0,4},{1,5},{2,6},{3,7},{4,0},{5,1},{6,2},{7,3},{8,12},{9,13},{10,... | collective-permute-start | bytes 786440 | tf_op jit(solution)/shard_map/ppermute | solution.py:301
  3.0 12.2 %collective-permute-start.2 = (f32[8,16,512]{2,1,0:T(8,128)}, f32[8,16,512]{2,1,0:T(8,128)S(1)}, u32[]{:S(2)}, u32[]{:S(2)}) collective-permute-start(f32[8,16,512]{2,1,0:T(8,128)} %right_ref.1), channel_id=1, source_target_pairs={{0,8},{1,9},{2,10},{3,11},{4,12},{5,13},{6,14},{7,15},{8,0},{9,1},... | collective-permute-start | bytes 786440 | tf_op jit(solution)/shard_map/ppermute | solution.py:301
  4.5 7.0 %collective-permute-start = (f32[4,16,512]{2,1,0:T(8,128)}, f32[4,16,512]{2,1,0:T(8,128)S(1)}, u32[]{:S(2)}, u32[]{:S(2)}) collective-permute-start(f32[4,16,512]{2,1,0:T(8,128)} %refs_0_.1), channel_id=1, source_target_pairs={{0,2},{1,3},{2,18},{3,19},{4,6},{5,7},{6,22},{7,23},{8,10},{9,11},... | collective-permute-start | bytes 393224 | tf_op jit(solution)/shard_map/ppermute | solution.py:301
  6.0 5.5 %collective-permute-start.3 = (f32[4,16,512]{2,1,0:T(8,128)}, f32[4,16,512]{2,1,0:T(8,128)S(1)}, u32[]{:S(2)}, u32[]{:S(2)}) collective-permute-start(f32[4,16,512]{2,1,0:T(8,128)} %refs_0_.1), channel_id=1, source_target_pairs={{0,1},{1,0},{2,3},{3,2},{4,5},{5,4},{6,7},{7,6},{8,9},{9,8},{10,11... | collective-permute-start | bytes 393224 | tf_op jit(solution)/shard_map/ppermute | solution.py:301
  6.0 19.1 %collective-permute-start.7 = (f32[8,16,512]{2,1,0:T(8,128)}, f32[8,16,512]{2,1,0:T(8,128)}, u32[]{:S(2)}, u32[]{:S(2)}) collective-permute-start(f32[8,16,512]{2,1,0:T(8,128)} %right_ref.1), channel_id=1, source_target_pairs={{0,12},{1,13},{2,14},{3,15},{4,8},{5,9},{6,10},{7,11},{8,4},{9,5},... | collective-permute-start | bytes 786440 | tf_op jit(solution)/shard_map/ppermute | solution.py:301
  6.4 0.9 %copy-start = (f32[4,16,512]{2,1,0:T(8,128)S(1)}, f32[4,16,512]{2,1,0:T(8,128)}, u32[]{:S(2)}) copy-start(f32[4,16,512]{2,1,0:T(8,128)} %refs_0_.1) | copy-start | bytes 393220
  7.3 0.9 %copy-start.4 = (f32[8,16,512]{2,1,0:T(8,128)S(1)}, f32[8,16,512]{2,1,0:T(8,128)}, u32[]{:S(2)}) copy-start(f32[8,16,512]{2,1,0:T(8,128)} %right_ref.1) | copy-start | bytes 786436
  8.3 0.9 %copy-start.9 = (f32[96,512]{1,0:T(8,128)S(1)}, f32[96,512]{1,0:T(8,128)}, u32[]{:S(2)}) copy-start(f32[96,512]{1,0:T(8,128)} %constant.36.clone.phases_ref) | copy-start | bytes 589828
  9.2 16.0 %copy-start.1 = (f32[4,16,512]{2,1,0:T(8,128)S(1)}, f32[4,16,512]{2,1,0:T(8,128)}, u32[]{:S(2)}) copy-start(f32[4,16,512]{2,1,0:T(8,128)} %refs_0_.1) | copy-start | bytes 393220
  10.7 0.8 %copy-start.2 = (f32[4,16,1536]{2,1,0:T(8,128)}, f32[4,16,1536]{2,1,0:T(8,128)S(1)}, u32[]{:S(2)}) copy-start(f32[4,16,1536]{2,1,0:T(8,128)S(1)} %get-tuple-element.51.here_ref) | copy-start | bytes 1179652
  15.2 0.7 %copy-start.7 = (f32[8,16,512]{2,1,0:T(8,128)}, f32[8,16,512]{2,1,0:T(8,128)S(1)}, u32[]{:S(2)}) copy-start(f32[8,16,512]{2,1,0:T(8,128)S(1)} %collective-permute-done.2.refs_1_) | copy-start | bytes 786436
  15.9 9.3 %collective-permute-start.4 = (f32[4,16,512]{2,1,0:T(8,128)S(1)}, f32[4,16,512]{2,1,0:T(8,128)S(1)}, u32[]{:S(2)}, u32[]{:S(2)}) collective-permute-start(f32[4,16,512]{2,1,0:T(8,128)S(1)} %collective-permute-done.one_ref.refs_1_), channel_id=1, source_target_pairs={{0,2},{1,3},{4,6},{5,7},{8,10},{9,11},{12,14},{13,15},{18,16},{19,... | collective-permute-start | bytes 393224 | tf_op jit(solution)/shard_map/ppermute | solution.py:301
  19.2 6.0 %collective-permute-start.5 = (f32[4,16,512]{2,1,0:T(8,128)S(1)}, f32[4,16,512]{2,1,0:T(8,128)S(1)}, u32[]{:S(2)}, u32[]{:S(2)}) collective-permute-start(f32[4,16,512]{2,1,0:T(8,128)S(1)} %collective-permute-done.one_ref.refs_1_), channel_id=1, source_target_pairs={{0,1},{1,0},{2,3},{3,2},{4,5},{5,4},{6,7},{7,6},{8,9},{9,8},{10,11... | collective-permute-start | bytes 393224 | tf_op jit(solution)/shard_map/ppermute | solution.py:301
  19.3 5.9 %collective-permute-start.6 = (f32[4,16,512]{2,1,0:T(8,128)S(1)}, f32[4,16,512]{2,1,0:T(8,128)S(1)}, u32[]{:S(2)}, u32[]{:S(2)}) collective-permute-start(f32[4,16,512]{2,1,0:T(8,128)S(1)} %collective-permute-done.one_ref.refs_1_), channel_id=1, source_target_pairs={{0,3},{1,2},{4,7},{5,6},{8,11},{9,10},{12,15},{13,14},{18,17},{19,... | collective-permute-start | bytes 393224 | tf_op jit(solution)/shard_map/ppermute | solution.py:301
  20.7 9.7 %copy-start.3 = (f32[4,16,1536]{2,1,0:T(8,128)S(1)}, f32[4,16,1536]{2,1,0:T(8,128)}, u32[]{:S(2)}) copy-start(f32[4,16,1536]{2,1,0:T(8,128)} %copy-done.2) | copy-start | bytes 1179652
  20.8 1.0 %copy-start.6 = (f32[8,16,512]{2,1,0:T(8,128)S(1)}, f32[8,16,512]{2,1,0:T(8,128)}, u32[]{:S(2)}) copy-start(f32[8,16,512]{2,1,0:T(8,128)} %copy-done.5) | copy-start | bytes 786436
  21.8 0.9 %copy-start.8 = (f32[8,16,512]{2,1,0:T(8,128)S(1)}, f32[8,16,512]{2,1,0:T(8,128)}, u32[]{:S(2)}) copy-start(f32[8,16,512]{2,1,0:T(8,128)} %copy-done.7) | copy-start | bytes 786436
  22.7 0.9 %copy-start.11 = (f32[3,21,4,16]{1,3,2,0:T(8,128)S(1)}, f32[3,21,4,16]{1,3,2,0:T(8,128)}, u32[]{:S(2)}) copy-start(f32[3,21,4,16]{1,3,2,0:T(8,128)} %param.9) | copy-start | bytes 48388
  25.8 8.7 %collective-permute-start.9 = (f32[2,32,512]{2,1,0:T(8,128)S(1)}, f32[2,32,512]{2,1,0:T(8,128)S(1)}, u32[]{:S(2)}, u32[]{:S(2)}) collective-permute-start(f32[2,32,512]{2,1,0:T(8,128)S(1)} %get-tuple-element.60), channel_id=1, source_target_pairs={{0,4},{1,5},{2,6},{3,7},{4,0},{5,1},{6,2},{7,3},{8,12},{9,13},{10,... | collective-permute-start | bytes 393224 | tf_op jit(solution)/shard_map/ppermute | solution.py:301
  26.4 8.1 %copy-start.12 = (s32[21]{0:T(128)S(1)}, s32[21]{0:T(128)}, u32[]{:S(2)}) copy-start(s32[21]{0:T(128)} %offsets_ref.3) | copy-start | bytes 256
  26.4 8.1 %collective-permute-start.10 = (f32[2,32,512]{2,1,0:T(8,128)S(1)}, f32[2,32,512]{2,1,0:T(8,128)S(1)}, u32[]{:S(2)}, u32[]{:S(2)}) collective-permute-start(f32[2,32,512]{2,1,0:T(8,128)S(1)} %get-tuple-element.61), channel_id=1, source_target_pairs={{0,12},{1,13},{2,14},{3,15},{4,8},{5,9},{6,10},{7,11},{8,4},{9,5},... | collective-permute-start | bytes 393224 | tf_op jit(solution)/shard_map/ppermute | solution.py:301
  28.5 5.9 %collective-permute-start.8 = (f32[64,128]{1,0:T(8,128)S(1)}, f32[64,128]{1,0:T(8,128)S(1)}, u32[]{:S(2)}, u32[]{:S(2)}) collective-permute-start(f32[64,128]{1,0:T(8,128)S(1)} %get-tuple-element.48.weights_ref), channel_id=1, source_target_pairs={{0,16},{1,17},{2,18},{3,19},{4,20},{5,21},{6,22},{7,23},{8,24},{9,... | collective-permute-start | bytes 98312 | tf_op jit(solution)/shard_map/ppermute | solution.py:301
  34.5 6.0 %copy-start.10 = (f32[4,16,512]{2,1,0:T(8,128)S(1)}, f32[4,16,512]{2,1,0:T(8,128)}, u32[]{:S(2)}) copy-start(f32[4,16,512]{2,1,0:T(8,128)} %recorded_ref.1) | copy-start | bytes 393220
  38.6 8.8 %collective-permute-start.11 = (f32[4,16,512]{2,1,0:T(8,128)S(1)}, f32[4,16,512]{2,1,0:T(8,128)S(1)}, u32[]{:S(2)}, u32[]{:S(2)}) collective-permute-start(f32[4,16,512]{2,1,0:T(8,128)S(1)} %get-tuple-element.64), channel_id=1, source_target_pairs={{0,16},{1,17},{2,18},{3,19},{4,20},{5,21},{6,22},{7,23},{8,24},{9,... | collective-permute-start | bytes 393224 | tf_op jit(solution)/shard_map/ppermute | solution.py:301
  (1 other events, 0.7 us)
where the time goes:
time: 48.4 us; the launch traced here: 48.1 us
  starting transfers between devices  17.7 us (37%)
  Pallas kernels  17.6 us (36%)
  local copies, waits for them, and re-layouts  7.75 us (16%)
  waiting for transfers between devices  4.83 us (10%)
    ppermute x12, starting transfers between devices, permute(): return lax.ppermute(array, AXES, pairs)  17.7 us
    pallas_call x7, Pallas kernels, call(): pl.pallas_call(kernel, out_shape=shapes, in_specs=[pl.BlockSpec(memory_sp...  17.6 us
    unnamed x26, local copies, waits for them, and re-layouts  7.75 us
    ppermute x12, waiting for transfers between devices, permute(): return lax.ppermute(array, AXES, pairs)  4.83 us
  transfers between devices with their start and end apart: 12, of which 3 were waited for; matrix products, arithmetic and copies ran while one was open for 0% of the time, Pallas kernels for 25%

commit v1 on v0

v1 whole, which is shorter than its diff:
```python
import functools
import math

import jax
import jax.numpy as jnp
import numpy as np
from jax import lax
from jax.experimental import pallas as pl
from jax.experimental.pallas import tpu as pltpu
from jax.sharding import PartitionSpec as P

LANES = 128
SUBLANES = 8
VMEM_LIMIT = 20 * 1024 * 1024
AXES = ("rcv", "src")
STEP = 32
GROUP = 4
CHUNK = 64


def phases(samples):
    fine = np.arange(STEP, dtype=np.int64)
    coarse = np.arange(0, samples, STEP, dtype=np.int64)
    times = np.concatenate([coarse, fine])[:, None]
    odd = 2 * np.arange(samples, dtype=np.int64)[None, :] + 1
    phase = (times * odd % (4 * samples)).astype(np.float64) * (math.pi / (2 * samples))
    return np.concatenate([np.cos(phase), np.sin(phase)], axis=0).astype(np.float32)


def dft_tables(high_ref, low_ref, phases_ref):
    samples = high_ref.shape[0]
    coarse = samples // STEP
    half = phases_ref.shape[0] // 2
    cos_fine = phases_ref[coarse:half]
    sin_fine = phases_ref[half + coarse :]
    for step in range(coarse):
        cos_step = phases_ref[step : step + 1]
        sin_step = phases_ref[half + step : half + step + 1]
        cosine = cos_step * cos_fine - sin_step * sin_fine
        sine = sin_step * cos_fine + cos_step * sin_fine
        for value, at in ((cosine, 0), (-sine, samples)):
            high = value.astype(jnp.bfloat16)
            where = (pl.ds(step * STEP, STEP), pl.ds(at, samples))
            high_ref[where] = high
            low_ref[where] = (value - high.astype(jnp.float32)).astype(jnp.bfloat16)


def split_dot(rows, high_table, low_table, of=0):
    high = rows.astype(jnp.bfloat16)
    low = (rows - high.astype(jnp.float32)).astype(jnp.bfloat16)

    def dot(left, right):
        return lax.dot_general(
            left, right, (((1,), (of,)), ((), ())), preferred_element_type=jnp.float32
        )

    return dot(high, high_table) + (dot(low, high_table) + dot(high, low_table))


def spectra(traces_ref, tables):
    lead = traces_ref.shape[:-1]
    samples = traces_ref.shape[-1]
    rows = math.prod(lead)
    return split_dot(traces_ref[...].reshape(rows, samples), *tables).reshape(lead + (2 * samples,))


def all_spectra(values, tables):
    rows = [math.prod(value.shape[:-1]) for value in values]
    samples = values[0].shape[-1]
    flat = split_dot(
        jnp.concatenate([value.reshape(-1, samples) for value in values]), *tables
    )
    starts = [sum(rows[:index]) for index in range(len(rows))]
    return [
        flat[start : start + count].reshape(value.shape[:-1] + (2 * samples,))
        for start, count, value in zip(starts, rows, values)
    ]


def with_sums(values):
    half = values.shape[-1] // 2
    total = values[..., :half] + values[..., half:]
    return jnp.concatenate([values, total], axis=-1)


def products(total_ref, lefts, right_ref):
    _, sources, width = total_ref.shape
    half = width // 2
    zero = jnp.zeros((sources, LANES), jnp.float32)
    for tile in range(half // LANES):
        real = pl.ds(tile * LANES, LANES)
        imag = pl.ds(half + tile * LANES, LANES)
        both = pl.ds(width + tile * LANES, LANES)
        for group in range(0, len(lefts), GROUP):
            members = lefts[group : group + GROUP]
            sums = [(zero, zero, zero) for _ in members]
            for bounce in range(right_ref.shape[0]):
                at = slice(bounce, bounce + 1)
                right_real = right_ref[bounce, :, real]
                right_imag = right_ref[bounce, :, imag]
                right_more = right_imag - right_real
                right_both = right_imag + right_real
                for index, (_, left_ref, row) in enumerate(members):
                    one, two, three = sums[index]
                    sums[index] = (
                        one + left_ref[row, at, both] * right_real,
                        two + left_ref[row, at, real] * right_more,
                        three + left_ref[row, at, imag] * right_both,
                    )
            for (one, two, three), (row, _, _) in zip(sums, members):
                total_ref[row, :, real] = one - three
                total_ref[row, :, imag] = one + two


def to_traces(prediction_ref, total_ref, tables):
    rows, sources, width = total_ref.shape
    flat = total_ref[...].reshape(rows * sources, width) * (2.0 / width)
    prediction_ref[...] = split_dot(flat, *tables, of=1).reshape(prediction_ref.shape)


def tap_rows(near, taps):
    inner = -(-near * taps // SUBLANES) * SUBLANES
    return inner, inner + -(-taps // SUBLANES) * SUBLANES


def lay_weights(weights_ref, scratch, filters_ref):
    near, receivers, sources, taps = filters_ref.shape
    inner, rows = tap_rows(near, taps)
    scratch[...] = jnp.zeros(scratch.shape, jnp.float32)
    lanes = receivers * sources
    for copy in range(LANES // lanes):
        for step in range(near):
            for row in range(receivers):
                receiver = row + 1 - step
                if 0 <= receiver < receivers:
                    at = pl.ds(copy * lanes + row * sources, sources)
                    scratch[at, step * taps : (step + 1) * taps] = filters_ref[step, receiver]
    for copy in range(LANES // (2 * sources)):
        for row, value in enumerate((filters_ref[0, 0], filters_ref[near - 1, receivers - 1])):
            at = pl.ds((copy * 2 + row) * sources, sources)
            scratch[at, inner : inner + taps] = value
    weights_ref[...] = scratch[...].T[:rows]


def turn(turned, prediction):
    receivers, sources, samples = prediction.shape
    lanes = receivers * sources
    per = samples * lanes // LANES
    zero = jnp.zeros((lanes, LANES), jnp.float32)
    for block in range(per // LANES + 2):
        side = []
        for start in range(0, samples, per):
            at = start + (block - 1) * LANES
            if 0 <= at < samples:
                side.append(prediction[:, :, at : at + LANES].reshape(lanes, LANES))
            else:
                side.append(zero)
        turned[pl.ds(block * LANES, LANES)] = jnp.concatenate(side, axis=0).T


def turn_back(value, receivers, sources):
    per = value.shape[0]
    parts = LANES // (receivers * sources)
    back = jnp.concatenate([value[at : at + LANES].T for at in range(0, per, LANES)], axis=1)
    back = back.reshape(parts, receivers, sources, per)
    return jnp.concatenate([back[part] for part in range(parts)], axis=2)


def matched(prediction, weights_ref, offsets_ref, turned, sums):
    receivers, sources, samples = prediction.shape
    near, taps = sums.shape[0], offsets_ref.shape[0]
    per = samples * receivers * sources // LANES
    turn(turned, prediction)
    chunk = min(per, CHUNK)
    for first in range(0, per, chunk):
        totals = [jnp.zeros((chunk, LANES), jnp.float32) for _ in range(near)]
        for tap in range(taps):
            shifted = turned[pl.ds(LANES + first - offsets_ref[tap], chunk), :]
            for step in range(near):
                at = step * taps + tap
                totals[step] = totals[step] + weights_ref[at : at + 1] * shifted
        for step in range(near):
            sums[step, pl.ds(first, chunk)] = totals[step]
    added = [None] * receivers
    for step in range(near):
        back = turn_back(sums[step, pl.ds(0, per)], receivers, sources)
        for row in range(receivers):
            receiver = row + 1 - step
            if 0 <= receiver < receivers:
                before = added[receiver]
                added[receiver] = back[row] if before is None else before + back[row]
    return added


def matched_halo(prediction, weights_ref, offsets_ref, turned):
    two, sources, samples = prediction.shape
    taps = offsets_ref.shape[0]
    first_tap = weights_ref.shape[0] - -(-taps // SUBLANES) * SUBLANES
    per = samples * two * sources // LANES
    turn(turned, prediction)
    total = jnp.zeros((per, LANES), jnp.float32)
    for tap in range(taps):
        shifted = turned[pl.ds(LANES - offsets_ref[tap], per), :]
        total = total + weights_ref[first_tap + tap : first_tap + tap + 1] * shifted
    return turn_back(total, two, sources)


def first_kernel(
    phases_ref, filters_ref, here_ref, right_ref,
    high_ref, low_ref, weights_ref, here_out, right_out, turned,
):
    dft_tables(high_ref, low_ref, phases_ref)
    lay_weights(weights_ref, turned, filters_ref)
    here, right = all_spectra(
        [here_ref[...], right_ref[...]], (high_ref[...], low_ref[...])
    )
    here_out[...] = with_sums(here)
    right_out[...] = right


def second_kernel(high_ref, low_ref, one_ref, *refs):
    right_refs, (one_out, right_out) = refs[:-2], refs[-2:]
    one, *right = all_spectra(
        [one_ref[...]] + [ref[...] for ref in right_refs], (high_ref[...], low_ref[...])
    )
    one_out[...] = with_sums(one)
    held = right_refs[0].shape[0]
    for block, value in enumerate(right):
        right_out[pl.ds(block * held, held)] = value


def position(slots, blocks):
    row, column = lax.axis_index("rcv"), lax.axis_index("src")
    return row, column, row // blocks == column // slots


def place_of(column, slot, slots, held):
    first = jnp.bitwise_xor(column, slot) % slots * held
    return pl.ds(pl.multiple_of(first, held), held)


def edge_kernel(slots, blocks, *refs):
    near_ref, far_ref = refs[3 * slots :]
    row, column, same = position(slots, blocks)
    odd = row % 2 == 1
    receivers, held, _ = refs[0].shape
    for slot in range(slots):
        these = place_of(column, slot, slots, held)
        here, one, two = refs[3 * slot : 3 * slot + 3]
        for index, (yes, no) in enumerate(((here, one), (one, two))):
            first = jnp.where(same, yes[0], no[0])
            last = jnp.where(same, yes[receivers - 1], no[receivers - 1])
            near_ref[index, these] = jnp.where(odd, first, last)
            far_ref[index, these] = jnp.where(odd, last, first)


def main_kernel(
    slots, blocks, offsets_from, high_ref, low_ref, weights_ref, right_a, right_b, one_ref, *refs
):
    columns, refs = refs[: 2 * slots - 1], refs[2 * slots - 1 :]
    right_refs, refs = refs[:-9], refs[-9:]
    out_ref, right_ref, total, prediction, turned, sums, offsets_ref, arrived, left_ref = refs
    copy = pltpu.make_async_copy(offsets_from, offsets_ref, arrived)
    copy.start()
    row, column, same = position(slots, blocks)
    count = right_a.shape[0]
    traces = [columns[0][...]]
    for slot in range(1, slots):
        one, two = columns[2 * slot - 1 : 2 * slot + 1]
        traces.append(jnp.where(same, one[...], two[...]))
    spectra_of = all_spectra(
        traces + [ref[...] for ref in right_refs], (high_ref[...], low_ref[...])
    )
    place = 0
    for value in [right_a, right_b] + spectra_of[slots:]:
        step = min(count, value.shape[0])
        for first in range(0, value.shape[0], step):
            at = jnp.bitwise_xor(row, place // count) % blocks * count + place % count
            right_ref[pl.ds(at, step)] = value[first : first + step]
            place += step
    receivers, held, _ = one_ref.shape
    for slot in range(slots):
        these = place_of(column, slot, slots, held)
        mirror = with_sums(spectra_of[slot])
        if slot == 0:
            mirror = jnp.where(same, one_ref[...], mirror)
        for receiver in range(receivers):
            left_ref[receiver, these] = mirror[receiver]
    products(total, [(row, left_ref, row) for row in range(receivers)], right_ref)
    to_traces(prediction, total, (high_ref[...], low_ref[...]))
    copy.wait()
    added = matched(prediction, weights_ref, offsets_ref, turned, sums)
    for receiver in range(receivers):
        out_ref[receiver] = added[receiver]


def mirror_kernel(
    blocks, offsets_from, high_ref, low_ref, weights_ref, near_ref, far_ref, part_ref,
    right_ref, out_ref, halo_ref, total, prediction, turned, offsets_ref, arrived, outer,
):
    copy = pltpu.make_async_copy(offsets_from, offsets_ref, arrived)
    copy.start()
    row = lax.axis_index("rcv")
    odd, lower = row % 2 == 1, row < blocks
    before = jnp.where(odd, near_ref[...], far_ref[...])
    after = jnp.where(odd, far_ref[...], near_ref[...])
    zero = jnp.zeros(before.shape[1:], jnp.float32)
    for which, (value, end, none) in enumerate(
        (
            (before, row % blocks == 0, lower),
            (after, row % blocks == blocks - 1, jnp.logical_not(lower)),
        )
    ):
        own, mirror = value[0], value[1]
        outer[which] = jnp.where(end, jnp.where(none, zero, mirror), own)
        outer[2 + which] = jnp.where(end, jnp.where(none, own, zero), mirror)
    tables = (high_ref[...], low_ref[...])
    halo_ref[...] = with_sums(spectra(outer, tables))
    products(total, [(0, halo_ref, 2), (1, halo_ref, 3)], right_ref)
    to_traces(prediction, total, tables)
    copy.wait()
    added = matched_halo(prediction[...], weights_ref, offsets_ref, turned)
    last = out_ref.shape[0] - 1
    out_ref[...] = part_ref[...]
    out_ref[0] = out_ref[0] + added[0]
    out_ref[last] = out_ref[last] + added[1]


def own_kernel(
    slots, blocks, offsets_from, high_ref, low_ref, weights_ref, right_ref, halo_ref,
    recorded_ref, here_ref, one_ref, *refs
):
    columns, refs = refs[: 2 * slots - 2], refs[2 * slots - 2 :]
    out_ref, total, prediction, turned, sums, offsets_ref, arrived, left_ref = refs
    copy = pltpu.make_async_copy(offsets_from, offsets_ref, arrived)
    copy.start()
    tables = (high_ref[...], low_ref[...])
    row, column, same = position(slots, blocks)
    receivers, held, _ = here_ref.shape
    for slot in range(slots):
        these = place_of(column, slot, slots, held)
        if slot == 0:
            own = jnp.where(same, here_ref[...], one_ref[...])
        else:
            here, one = columns[2 * slot - 2 : 2 * slot]
            chosen = jnp.where(same, here[...], one[...])
            own = with_sums(all_spectra([chosen], tables)[0])
        for receiver in range(receivers):
            left_ref[receiver, these] = own[receiver]
    lefts = [(row, left_ref, row) for row in range(receivers)]
    lefts += [(receivers, halo_ref, 0), (receivers + 1, halo_ref, 1)]
    products(total, lefts, right_ref)
    to_traces(prediction, total, tables)
    copy.wait()
    last = receivers - 1
    added = matched(prediction[:receivers], weights_ref, offsets_ref, turned, sums)
    outer = matched_halo(prediction[receivers:], weights_ref, offsets_ref, turned)
    for receiver in range(receivers):
        value = recorded_ref[receiver] - added[receiver]
        if receiver == 0:
            value = value - outer[0]
        if receiver == last:
            value = value - outer[1]
        out_ref[receiver] = value


def last_kernel(part_ref, arrived_ref, out_ref):
    out_ref[...] = part_ref[...] - arrived_ref[...]


def call(kernel, arrays, outs, scratch, in_place=0):
    shapes = [s if hasattr(s, "dtype") else jax.ShapeDtypeStruct(s, jnp.float32) for s in outs]
    vmem = pl.BlockSpec(memory_space=pltpu.VMEM)
    return pl.pallas_call(
        kernel,
        out_shape=shapes,
        in_specs=[pl.BlockSpec(memory_space=pl.ANY)] * in_place + [vmem] * (len(arrays) - in_place),
        out_specs=[vmem] * len(shapes),
        scratch_shapes=[
            s if not isinstance(s, tuple) else pltpu.VMEM(s, jnp.float32) for s in scratch
        ],
        compiler_params=pltpu.CompilerParams(vmem_limit_bytes=VMEM_LIMIT),
    )(*arrays)


def local(rows, columns, rb_data, bs_data, recorded, filters, offsets):
    receivers, left_count, samples = rb_data.shape
    right_count, sources, _ = bs_data.shape
    near_count, taps = filters.shape[:2]
    slots, blocks = columns // 2, rows // 2
    def permute(array, target):
        pairs = []
        for i in range(rows):
            for j in range(columns):
                to = target(i, j)
                if to is not None:
                    pairs.append((i * columns + j, to[0] * columns + to[1]))
        return lax.ppermute(array, AXES, pairs)

    def is_same(i, j):
        return i // blocks == j // slots

    cut = 2 * blocks // 3 + 1
    width = 2 * samples
    held = slots * left_count
    one = permute(
        rb_data, lambda i, j: (i, j ^ slots) if is_same(i, j) else (i ^ blocks, j)
    )
    some = [permute(bs_data, lambda i, j, k=k: (i ^ k, j)) for k in range(1, cut)]
    heres = [rb_data] + [
        permute(rb_data, lambda i, j, k=k: (i, j ^ k)) for k in range(1, slots)
    ]
    table = jax.ShapeDtypeStruct((samples, width), jnp.bfloat16)
    left_shape = (receivers, left_count, width + samples)
    high, low, weights, here_spectra, right_a = call(
        first_kernel,
        [jnp.asarray(phases(samples)), filters.transpose(0, 2, 3, 1), rb_data, bs_data],
        [
            table, table, (tap_rows(near_count, taps)[1], LANES), left_shape,
            (right_count, sources, width),
        ],
        [(LANES, LANES)],
    )
    one, some, heres, high, low, weights, here_spectra, right_a = lax.optimization_barrier(
        (one, some, heres, high, low, weights, here_spectra, right_a)
    )
    two = permute(one, lambda i, j: (i, j ^ slots) if is_same(i, j) else None)
    ones = [permute(one, lambda i, j, k=k: (i, j ^ k)) for k in range(1, slots)]
    rest = []
    for k in range(cut, blocks):
        bits = [1 << n for n in range(blocks) if 0 < k ^ (1 << n) < cut][:2]
        part = right_count // len(bits)
        for n, bit in enumerate(bits):
            of = some[(k ^ bit) - 1][n * part : (n + 1) * part if n + 1 < len(bits) else None]
            rest.append(permute(of, lambda i, j, bit=bit: (i ^ bit, j)))
    mirror_weights = permute(weights, lambda i, j: (i ^ blocks, j))
    one_spectra, right_b = call(
        second_kernel, [high, low, one] + some,
        [left_shape, (len(some) * right_count, sources, width)], [],
    )
    two, ones, mirror_weights, one_spectra, right_b = lax.optimization_barrier(
        (two, ones, mirror_weights, one_spectra, right_b)
    )
    gathered = [two]
    for k in range(1, slots):
        gathered += [heres[k], ones[k - 1]]
        gathered.append(permute(two, lambda i, j, k=k: None if is_same(i, j) else (i, j ^ k)))
    gathered, rest = lax.optimization_barrier((gathered, rest))
    edge_shape = (2, held, samples)
    near, far = call(
        functools.partial(edge_kernel, slots, blocks), [rb_data, one] + gathered,
        [edge_shape, edge_shape], [],
    )

    def in_half(i, at):
        return at % blocks + i // blocks * blocks

    near = permute(near, lambda i, j: (i ^ 1, j))
    far = permute(far, lambda i, j: (in_half(i, i + 1 if i % 2 else i - 1), j))
    per = samples * receivers * sources // LANES
    right_shape = (blocks * right_count, sources, width)
    own_shape = (receivers, held, width + samples)

    def scratch_of(predicted):
        return [(predicted, sources, width), (predicted, sources, samples), (per + 2 * LANES, LANES)]

    sums = [(near_count, per, LANES)]
    taken = [pltpu.SMEM(offsets.shape, jnp.int32), pltpu.SemaphoreType.DMA(())]
    ones_twos = [two]
    heres_ones = []
    for k in range(1, slots):
        ones_twos += gathered[3 * k - 1 : 3 * k + 1]
        heres_ones += gathered[3 * k - 2 : 3 * k]
    part, right = call(
        functools.partial(main_kernel, slots, blocks),
        [offsets, high, low, mirror_weights, right_a, right_b, one_spectra] + ones_twos + rest,
        [recorded.shape, right_shape],
        scratch_of(receivers) + sums + taken + [own_shape],
        in_place=1,
    )
    mirror_part, halo = call(
        functools.partial(mirror_kernel, blocks),
        [offsets, high, low, mirror_weights, near, far, part, right],
        [recorded.shape, (4, held, width + samples)],
        scratch_of(2) + taken + [(4, held, samples)],
        in_place=1,
    )
    arrived = permute(mirror_part, lambda i, j: (i ^ blocks, j))
    (own_part,) = call(
        functools.partial(own_kernel, slots, blocks),
        [offsets, high, low, weights, right, halo, recorded, here_spectra, one_spectra]
        + heres_ones,
        [recorded.shape],
        scratch_of(receivers + 2) + sums + taken + [own_shape],
        in_place=1,
    )
    (out,) = call(last_kernel, [own_part, arrived], [recorded.shape], [])
    return out


def solution(mesh):
    in_specs = (
        P("rcv", "src", None),
        P("rcv", "src", None),
        P("rcv", "src", None),
        P(None, None, "rcv", "src"),
        P(),
    )
    out_specs = P("rcv", "src", None)
    body = functools.partial(local, mesh.shape["rcv"], mesh.shape["src"])
    return jax.shard_map(body, mesh=mesh, in_specs=in_specs, out_specs=out_specs, check_vma=False)
```

time: 48.4 us -> 42.8 us (0.88)
  local copies, waits for them, and re-layouts: 7.75 us -> 3.73 us
  waiting for transfers between devices: 4.83 us -> 8.54 us
  Pallas kernels: 17.6 us -> 14.2 us
  starting transfers between devices: 17.7 us -> 16 us
    unnamed x26 -> x12, local copies, waits for them, and re-layouts: 7.75 us -> 3.71 us
    ppermute x12 -> x13, waiting for transfers between devices: 4.83 us -> 8.54 us  [permute(): return lax.ppermute(array, AXES, pairs)]
    pallas_call x7, Pallas kernels: 17.6 us -> 14.2 us  [call(): pl.pallas_call(kernel, out_shape=shapes, in_specs=[pl.BlockSpec(memory_sp...]
    ppermute x12 -> x13, starting transfers between devices: 17.7 us -> 16 us  [permute(): return lax.ppermute(array, AXES, pairs)]
  transfers between devices with their start and end apart: 12 -> 13, of which waited for: 3 -> 5; matrix products, arithmetic and copies ran while one was open for 0% -> 0% of each run, Pallas kernels for 25% -> 26%
where the time goes in v1:
time: 42.8 us; the launch traced here: 42.6 us
  starting transfers between devices  16 us (37%)
  Pallas kernels  14.2 us (33%)
  waiting for transfers between devices  8.54 us (20%)
  local copies, waits for them, and re-layouts  3.73 us (9%)
    ppermute x13, starting transfers between devices, permute(): return lax.ppermute(array, AXES, pairs)  16 us
    pallas_call x7, Pallas kernels, call(): pl.pallas_call(kernel, out_shape=shapes, in_specs=[pl.BlockSpec(memory_sp...  14.2 us
    ppermute x13, waiting for transfers between devices, permute(): return lax.ppermute(array, AXES, pairs)  8.54 us
    unnamed x12, local copies, waits for them, and re-layouts  3.71 us
  transfers between devices with their start and end apart: 13, of which 5 were waited for; matrix products, arithmetic and copies ran while one was open for 0% of the time, Pallas kernels for 26%

profile of v1, /device:TPU:0, one launch (start us, length us, event | category | flops | bytes accessed | tf_op | source)
XLA Modules:
  0.0 42.6 jit_solution(13885201018641498109)
XLA Ops:
  0.0 3.0 %collective-permute-start.1 = (f32[8,16,512]{2,1,0:T(8,128)}, f32[8,16,512]{2,1,0:T(8,128)S(1)}, u32[]{:S(2)}, u32[]{:S(2)}) collective-permute-start(f32[8,16,512]{2,1,0:T(8,128)} %right_ref.1), channel_id=1, source_target_pairs={{0,4},{1,5},{2,6},{3,7},{4,0},{5,1},{6,2},{7,3},{8,12},{9,13},{10,... | collective-permute-start | bytes 786440 | tf_op jit(solution)/shard_map/ppermute | solution.py:398
  3.0 1.6 %collective-permute-start.2 = (f32[8,16,512]{2,1,0:T(8,128)}, f32[8,16,512]{2,1,0:T(8,128)S(1)}, u32[]{:S(2)}, u32[]{:S(2)}) collective-permute-start(f32[8,16,512]{2,1,0:T(8,128)} %right_ref.1), channel_id=1, source_target_pairs={{0,8},{1,9},{2,10},{3,11},{4,12},{5,13},{6,14},{7,15},{8,0},{9,1},... | collective-permute-start | bytes 786440 | tf_op jit(solution)/shard_map/ppermute | solution.py:398
  4.5 1.5 %collective-permute-start = (f32[4,16,512]{2,1,0:T(8,128)}, f32[4,16,512]{2,1,0:T(8,128)S(1)}, u32[]{:S(2)}, u32[]{:S(2)}) collective-permute-start(f32[4,16,512]{2,1,0:T(8,128)} %refs_0_.1), channel_id=1, source_target_pairs={{0,2},{1,3},{2,18},{3,19},{4,6},{5,7},{6,22},{7,23},{8,10},{9,11},... | collective-permute-start | bytes 393224 | tf_op jit(solution)/shard_map/ppermute | solution.py:398
  6.0 0.9 %copy-done = f32[4,16,512]{2,1,0:T(8,128)S(1)} copy-done((f32[4,16,512]{2,1,0:T(8,128)S(1)}, f32[4,16,512]{2,1,0:T(8,128)}, u32[]{:S(2)}) %copy-start) | copy-done | bytes 131096
  7.0 0.9 %copy-done.1 = f32[8,16,512]{2,1,0:T(8,128)S(1)} copy-done((f32[8,16,512]{2,1,0:T(8,128)S(1)}, f32[8,16,512]{2,1,0:T(8,128)}, u32[]{:S(2)}) %copy-start.1) | copy-done | bytes 262168
  7.9 0.9 %copy-done.2 = f32[96,512]{1,0:T(8,128)S(1)} copy-done((f32[96,512]{1,0:T(8,128)S(1)}, f32[96,512]{1,0:T(8,128)}, u32[]{:S(2)}) %copy-start.2) | copy-done | bytes 196632
  8.9 0.9 %copy-done.4 = f32[3,21,4,16]{1,3,2,0:T(8,128)S(1)} copy-done((f32[3,21,4,16]{1,3,2,0:T(8,128)S(1)}, f32[3,21,4,16]{1,3,2,0:T(8,128)}, u32[]{:S(2)}) %copy-start.4) | copy-done | bytes 16152
  9.7 1.2 %shard_map.64 = (bf16[512,1024]{1,0:T(8,128)(2,1)S(1)}, bf16[512,1024]{1,0:T(8,128)(2,1)S(1)}, f32[88,128]{1,0:T(8,128)S(1)}, f32[4,16,1536]{2,1,0:T(8,128)S(1)}, f32[8,16,1024]{2,1,0:T(8,128)S(1)}) custom-call(f32[96,512]{1,0:T(8,128)S(1)} %copy-done.2, f32[3,4,16,21]{3,2,1,0:T(8,128)S(1)} %bitcast.1, f32[4,16,512]{2,1,0:T(8,128)S(1)} %copy-done, ...), custom_call_target="tpu_custom_call" | custom-call | tf_op jit(solution)/shard_map/pallas_call | solution.py:374
  11.0 2.8 %collective-permute-done.2.refs_1_ = f32[8,16,512]{2,1,0:T(8,128)S(1)} collective-permute-done((f32[8,16,512]{2,1,0:T(8,128)}, f32[8,16,512]{2,1,0:T(8,128)S(1)}, u32[]{:S(2)}, u32[]{:S(2)}) %collective-permute-start.2) | collective-permute-done | bytes 262176 | tf_op jit(solution)/shard_map/ppermute | solution.py:398
  13.8 2.6 %collective-permute-start.4 = (f32[4,16,512]{2,1,0:T(8,128)S(1)}, f32[4,16,512]{2,1,0:T(8,128)S(1)}, u32[]{:S(2)}, u32[]{:S(2)}) collective-permute-start(f32[4,16,512]{2,1,0:T(8,128)S(1)} %collective-permute-done.one_ref.refs_1_), channel_id=1, source_target_pairs={{0,2},{1,3},{4,6},{5,7},{8,10},{9,11},{12,14},{13,15},{18,16},{19,... | collective-permute-start | bytes 393224 | tf_op jit(solution)/shard_map/ppermute | solution.py:398
  16.6 0.6 %collective-permute-start.8 = (f32[4,16,512]{2,1,0:T(8,128)S(1)}, f32[4,16,512]{2,1,0:T(8,128)S(1)}, u32[]{:S(2)}, u32[]{:S(2)}) collective-permute-start(f32[4,16,512]{2,1,0:T(8,128)S(1)} %slice.6), channel_id=1, source_target_pairs={{0,4},{1,5},{2,6},{3,7},{4,0},{5,1},{6,2},{7,3},{8,12},{9,13},{10,... | collective-permute-start | bytes 393224 | tf_op jit(solution)/shard_map/ppermute | solution.py:398
  17.1 1.3 %collective-permute-start.9 = (f32[4,16,512]{2,1,0:T(8,128)S(1)}, f32[4,16,512]{2,1,0:T(8,128)S(1)}, u32[]{:S(2)}, u32[]{:S(2)}) collective-permute-start(f32[4,16,512]{2,1,0:T(8,128)S(1)} %slice.7), channel_id=1, source_target_pairs={{0,8},{1,9},{2,10},{3,11},{4,12},{5,13},{6,14},{7,15},{8,0},{9,1},... | collective-permute-start | bytes 393224 | tf_op jit(solution)/shard_map/ppermute | solution.py:398
  18.5 1.2 %shard_map.65 = (f32[4,16,1536]{2,1,0:T(8,128)S(1)}, f32[16,16,1024]{2,1,0:T(8,128)S(1)}) custom-call(bf16[512,1024]{1,0:T(8,128)(2,1)S(1)} %get-tuple-element.43.high_ref, bf16[512,1024]{1,0:T(8,128)(2,1)S(1)} %get-tuple-element.44.low_ref, f32[4,16,512]{2,1,0:T(8,128)S(1)} %collective-permute-done.one_ref.refs_1_, ...), custom_call_target="tpu_custom_call" | custom-call | tf_op jit(solution)/shard_map/pallas_call | solution.py:374
  19.7 2.9 %collective-permute-done.6.weights_ref = f32[88,128]{1,0:T(8,128)S(1)} collective-permute-done((f32[88,128]{1,0:T(8,128)S(1)}, f32[88,128]{1,0:T(8,128)S(1)}, u32[]{:S(2)}, u32[]{:S(2)}) %collective-permute-start.6) | collective-permute-done | bytes 45088 | tf_op jit(solution)/shard_map/ppermute | solution.py:398
  22.5 0.7 %collective-permute-start.7 = (f32[4,16,512]{2,1,0:T(8,128)S(1)}, f32[4,16,512]{2,1,0:T(8,128)S(1)}, u32[]{:S(2)}, u32[]{:S(2)}) collective-permute-start(f32[4,16,512]{2,1,0:T(8,128)S(1)} %collective-permute-done.4.refs_0_.refs_2_), channel_id=1, source_target_pairs={{2,3},{3,2},{6,7},{7,6},{10,11},{11,10},{14,15},{15,14},{16,17},{1... | collective-permute-start | bytes 393224 | tf_op jit(solution)/shard_map/ppermute | solution.py:398
  23.2 0.5 %collective-permute-done.9.refs_4_ = f32[4,16,512]{2,1,0:T(8,128)S(1)} collective-permute-done((f32[4,16,512]{2,1,0:T(8,128)S(1)}, f32[4,16,512]{2,1,0:T(8,128)S(1)}, u32[]{:S(2)}, u32[]{:S(2)}) %collective-permute-start.9) | collective-permute-done | bytes 131104 | tf_op jit(solution)/shard_map/ppermute | solution.py:398
  23.8 1.1 %collective-permute-start.10 = (f32[2,32,512]{2,1,0:T(8,128)S(1)}, f32[2,32,512]{2,1,0:T(8,128)S(1)}, u32[]{:S(2)}, u32[]{:S(2)}) collective-permute-start(f32[2,32,512]{2,1,0:T(8,128)S(1)} %get-tuple-element.65), channel_id=1, source_target_pairs={{0,4},{1,5},{2,6},{3,7},{4,0},{5,1},{6,2},{7,3},{8,12},{9,13},{10,... | collective-permute-start | bytes 393224 | tf_op jit(solution)/shard_map/ppermute | solution.py:398
  24.9 0.7 %collective-permute-start.11 = (f32[2,32,512]{2,1,0:T(8,128)S(1)}, f32[2,32,512]{2,1,0:T(8,128)S(1)}, u32[]{:S(2)}, u32[]{:S(2)}) collective-permute-start(f32[2,32,512]{2,1,0:T(8,128)S(1)} %get-tuple-element.66), channel_id=1, source_target_pairs={{0,12},{1,13},{2,14},{3,15},{4,8},{5,9},{6,10},{7,11},{8,4},{9,5},... | collective-permute-start | bytes 393224 | tf_op jit(solution)/shard_map/ppermute | solution.py:398
  25.6 4.0 %shard_map.66 = (f32[4,16,512]{2,1,0:T(8,128)S(1)}, f32[32,16,1024]{2,1,0:T(8,128)S(1)}) custom-call(s32[21]{0:T(128)S(1)} %copy-done.5, bf16[512,1024]{1,0:T(8,128)(2,1)S(1)} %get-tuple-element.43.high_ref, bf16[512,1024]{1,0:T(8,128)(2,1)S(1)} %get-tuple-element.44.low_ref, f32[88,128]{1,0:T(8,128)S(1)} %collective-permute-done.6.weights_ref, ...), custom_call_target="tpu_custom_call" | custom-call | tf_op jit(solution)/shard_map/pallas_call | solution.py:374
  29.6 2.0 %collective-permute-done.10.near_ref = f32[2,32,512]{2,1,0:T(8,128)S(1)} collective-permute-done((f32[2,32,512]{2,1,0:T(8,128)S(1)}, f32[2,32,512]{2,1,0:T(8,128)S(1)}, u32[]{:S(2)}, u32[]{:S(2)}) %collective-permute-start.10) | collective-permute-done | bytes 131104 | tf_op jit(solution)/shard_map/ppermute | solution.py:398
  31.6 2.3 %shard_map.68 = (f32[4,16,512]{2,1,0:T(8,128)S(1)}, f32[4,32,1536]{2,1,0:T(8,128)S(1)}) custom-call(s32[21]{0:T(128)S(1)} %copy-done.5, bf16[512,1024]{1,0:T(8,128)(2,1)S(1)} %get-tuple-element.43.high_ref, bf16[512,1024]{1,0:T(8,128)(2,1)S(1)} %get-tuple-element.44.low_ref, f32[88,128]{1,0:T(8,128)S(1)} %collective-permute-done.6.weights_ref, ...), custom_call_target="tpu_custom_call" | custom-call | tf_op jit(solution)/shard_map/pallas_call | solution.py:374
  34.0 2.8 %collective-permute-start.12 = (f32[4,16,512]{2,1,0:T(8,128)S(1)}, f32[4,16,512]{2,1,0:T(8,128)S(1)}, u32[]{:S(2)}, u32[]{:S(2)}) collective-permute-start(f32[4,16,512]{2,1,0:T(8,128)S(1)} %get-tuple-element.70), channel_id=1, source_target_pairs={{0,16},{1,17},{2,18},{3,19},{4,20},{5,21},{6,22},{7,23},{8,24},{9,... | collective-permute-start | bytes 393224 | tf_op jit(solution)/shard_map/ppermute | solution.py:398
  36.7 4.8 %shard_map.69.part_ref = f32[4,16,512]{2,1,0:T(8,128)S(1)} custom-call(s32[21]{0:T(128)S(1)} %copy-done.5, bf16[512,1024]{1,0:T(8,128)(2,1)S(1)} %get-tuple-element.43.high_ref, bf16[512,1024]{1,0:T(8,128)(2,1)S(1)} %get-tuple-element.44.low_ref, f32[88,128]{1,0:T(8,128)S(1)} %get-tuple-element.45.weights_ref, ...), custom_call_target="tpu_custom_call" | custom-call | tf_op jit(solution)/shard_map/pallas_call | solution.py:374
  41.9 0.7 %shard_map.70 = f32[4,16,512]{2,1,0:T(8,128)} custom-call(f32[4,16,512]{2,1,0:T(8,128)S(1)} %shard_map.69.part_ref, f32[4,16,512]{2,1,0:T(8,128)S(1)} %collective-permute-done.12.arrived_ref), custom_call_target="tpu_custom_call" | custom-call | tf_op jit(solution)/shard_map/pallas_call | solution.py:374
  (23 shorter events, 0.6 us)
Async XLA Ops:
  0.0 11.0 %collective-permute-start.1 = (f32[8,16,512]{2,1,0:T(8,128)}, f32[8,16,512]{2,1,0:T(8,128)S(1)}, u32[]{:S(2)}, u32[]{:S(2)}) collective-permute-start(f32[8,16,512]{2,1,0:T(8,128)} %right_ref.1), channel_id=1, source_target_pairs={{0,4},{1,5},{2,6},{3,7},{4,0},{5,1},{6,2},{7,3},{8,12},{9,13},{10,... | collective-permute-start | bytes 786440 | tf_op jit(solution)/shard_map/ppermute | solution.py:398
  3.0 10.8 %collective-permute-start.2 = (f32[8,16,512]{2,1,0:T(8,128)}, f32[8,16,512]{2,1,0:T(8,128)S(1)}, u32[]{:S(2)}, u32[]{:S(2)}) collective-permute-start(f32[8,16,512]{2,1,0:T(8,128)} %right_ref.1), channel_id=1, source_target_pairs={{0,8},{1,9},{2,10},{3,11},{4,12},{5,13},{6,14},{7,15},{8,0},{9,1},... | collective-permute-start | bytes 786440 | tf_op jit(solution)/shard_map/ppermute | solution.py:398
  4.5 6.4 %collective-permute-start = (f32[4,16,512]{2,1,0:T(8,128)}, f32[4,16,512]{2,1,0:T(8,128)S(1)}, u32[]{:S(2)}, u32[]{:S(2)}) collective-permute-start(f32[4,16,512]{2,1,0:T(8,128)} %refs_0_.1), channel_id=1, source_target_pairs={{0,2},{1,3},{2,18},{3,19},{4,6},{5,7},{6,22},{7,23},{8,10},{9,11},... | collective-permute-start | bytes 393224 | tf_op jit(solution)/shard_map/ppermute | solution.py:398
  6.0 4.9 %collective-permute-start.3 = (f32[4,16,512]{2,1,0:T(8,128)}, f32[4,16,512]{2,1,0:T(8,128)S(1)}, u32[]{:S(2)}, u32[]{:S(2)}) collective-permute-start(f32[4,16,512]{2,1,0:T(8,128)} %refs_0_.1), channel_id=1, source_target_pairs={{0,1},{1,0},{2,3},{3,2},{4,5},{5,4},{6,7},{7,6},{8,9},{9,8},{10,11... | collective-permute-start | bytes 393224 | tf_op jit(solution)/shard_map/ppermute | solution.py:398
  6.0 0.9 %copy-start = (f32[4,16,512]{2,1,0:T(8,128)S(1)}, f32[4,16,512]{2,1,0:T(8,128)}, u32[]{:S(2)}) copy-start(f32[4,16,512]{2,1,0:T(8,128)} %refs_0_.1) | copy-start | bytes 393220
  7.0 0.9 %copy-start.1 = (f32[8,16,512]{2,1,0:T(8,128)S(1)}, f32[8,16,512]{2,1,0:T(8,128)}, u32[]{:S(2)}) copy-start(f32[8,16,512]{2,1,0:T(8,128)} %right_ref.1) | copy-start | bytes 786436
  7.9 0.9 %copy-start.2 = (f32[96,512]{1,0:T(8,128)S(1)}, f32[96,512]{1,0:T(8,128)}, u32[]{:S(2)}) copy-start(f32[96,512]{1,0:T(8,128)} %constant.2.clone.phases_ref) | copy-start | bytes 589828
  8.9 0.9 %copy-start.4 = (f32[3,21,4,16]{1,3,2,0:T(8,128)S(1)}, f32[3,21,4,16]{1,3,2,0:T(8,128)}, u32[]{:S(2)}) copy-start(f32[3,21,4,16]{1,3,2,0:T(8,128)} %param.9) | copy-start | bytes 48388
  10.9 14.7 %copy-start.5 = (s32[21]{0:T(128)S(1)}, s32[21]{0:T(128)}, u32[]{:S(2)}) copy-start(s32[21]{0:T(128)} %offsets_from.5) | copy-start | bytes 256
  13.8 8.8 %collective-permute-start.4 = (f32[4,16,512]{2,1,0:T(8,128)S(1)}, f32[4,16,512]{2,1,0:T(8,128)S(1)}, u32[]{:S(2)}, u32[]{:S(2)}) collective-permute-start(f32[4,16,512]{2,1,0:T(8,128)S(1)} %collective-permute-done.one_ref.refs_1_), channel_id=1, source_target_pairs={{0,2},{1,3},{4,6},{5,7},{8,10},{9,11},{12,14},{13,15},{18,16},{19,... | collective-permute-start | bytes 393224 | tf_op jit(solution)/shard_map/ppermute | solution.py:398
  16.4 6.2 %collective-permute-start.5 = (f32[4,16,512]{2,1,0:T(8,128)S(1)}, f32[4,16,512]{2,1,0:T(8,128)S(1)}, u32[]{:S(2)}, u32[]{:S(2)}) collective-permute-start(f32[4,16,512]{2,1,0:T(8,128)S(1)} %collective-permute-done.one_ref.refs_1_), channel_id=1, source_target_pairs={{0,1},{1,0},{2,3},{3,2},{4,5},{5,4},{6,7},{7,6},{8,9},{9,8},{10,11... | collective-permute-start | bytes 393224 | tf_op jit(solution)/shard_map/ppermute | solution.py:398
  16.5 6.1 %collective-permute-start.6 = (f32[88,128]{1,0:T(8,128)S(1)}, f32[88,128]{1,0:T(8,128)S(1)}, u32[]{:S(2)}, u32[]{:S(2)}) collective-permute-start(f32[88,128]{1,0:T(8,128)S(1)} %get-tuple-element.45.weights_ref), channel_id=1, source_target_pairs={{0,16},{1,17},{2,18},{3,19},{4,20},{5,21},{6,22},{7,23},{8,24},{9,... | collective-permute-start | bytes 135176 | tf_op jit(solution)/shard_map/ppermute | solution.py:398
  16.6 6.7 %collective-permute-start.8 = (f32[4,16,512]{2,1,0:T(8,128)S(1)}, f32[4,16,512]{2,1,0:T(8,128)S(1)}, u32[]{:S(2)}, u32[]{:S(2)}) collective-permute-start(f32[4,16,512]{2,1,0:T(8,128)S(1)} %slice.6), channel_id=1, source_target_pairs={{0,4},{1,5},{2,6},{3,7},{4,0},{5,1},{6,2},{7,3},{8,12},{9,13},{10,... | collective-permute-start | bytes 393224 | tf_op jit(solution)/shard_map/ppermute | solution.py:398
  17.1 6.6 %collective-permute-start.9 = (f32[4,16,512]{2,1,0:T(8,128)S(1)}, f32[4,16,512]{2,1,0:T(8,128)S(1)}, u32[]{:S(2)}, u32[]{:S(2)}) collective-permute-start(f32[4,16,512]{2,1,0:T(8,128)S(1)} %slice.7), channel_id=1, source_target_pairs={{0,8},{1,9},{2,10},{3,11},{4,12},{5,13},{6,14},{7,15},{8,0},{9,1},... | collective-permute-start | bytes 393224 | tf_op jit(solution)/shard_map/ppermute | solution.py:398
  22.5 1.2 %collective-permute-start.7 = (f32[4,16,512]{2,1,0:T(8,128)S(1)}, f32[4,16,512]{2,1,0:T(8,128)S(1)}, u32[]{:S(2)}, u32[]{:S(2)}) collective-permute-start(f32[4,16,512]{2,1,0:T(8,128)S(1)} %collective-permute-done.4.refs_0_.refs_2_), channel_id=1, source_target_pairs={{2,3},{3,2},{6,7},{7,6},{10,11},{11,10},{14,15},{15,14},{16,17},{1... | collective-permute-start | bytes 393224 | tf_op jit(solution)/shard_map/ppermute | solution.py:398
  23.8 7.8 %collective-permute-start.10 = (f32[2,32,512]{2,1,0:T(8,128)S(1)}, f32[2,32,512]{2,1,0:T(8,128)S(1)}, u32[]{:S(2)}, u32[]{:S(2)}) collective-permute-start(f32[2,32,512]{2,1,0:T(8,128)S(1)} %get-tuple-element.65), channel_id=1, source_target_pairs={{0,4},{1,5},{2,6},{3,7},{4,0},{5,1},{6,2},{7,3},{8,12},{9,13},{10,... | collective-permute-start | bytes 393224 | tf_op jit(solution)/shard_map/ppermute | solution.py:398
  24.9 6.7 %collective-permute-start.11 = (f32[2,32,512]{2,1,0:T(8,128)S(1)}, f32[2,32,512]{2,1,0:T(8,128)S(1)}, u32[]{:S(2)}, u32[]{:S(2)}) collective-permute-start(f32[2,32,512]{2,1,0:T(8,128)S(1)} %get-tuple-element.66), channel_id=1, source_target_pairs={{0,12},{1,13},{2,14},{3,15},{4,8},{5,9},{6,10},{7,11},{8,4},{9,5},... | collective-permute-start | bytes 393224 | tf_op jit(solution)/shard_map/ppermute | solution.py:398
  31.6 5.1 %copy-start.3 = (f32[4,16,512]{2,1,0:T(8,128)S(1)}, f32[4,16,512]{2,1,0:T(8,128)}, u32[]{:S(2)}) copy-start(f32[4,16,512]{2,1,0:T(8,128)} %recorded_ref.1) | copy-start | bytes 393220
  34.0 7.9 %collective-permute-start.12 = (f32[4,16,512]{2,1,0:T(8,128)S(1)}, f32[4,16,512]{2,1,0:T(8,128)S(1)}, u32[]{:S(2)}, u32[]{:S(2)}) collective-permute-start(f32[4,16,512]{2,1,0:T(8,128)S(1)} %get-tuple-element.70), channel_id=1, source_target_pairs={{0,16},{1,17},{2,18},{3,19},{4,20},{5,21},{6,22},{7,23},{8,24},{9,... | collective-permute-start | bytes 393224 | tf_op jit(solution)/shard_map/ppermute | solution.py:398

commit v2 on v1

--- a/solution.py
+++ b/solution.py
@@ -14,7 +14,7 @@
 VMEM_LIMIT = 20 * 1024 * 1024
 AXES = ("rcv", "src")
 STEP = 32
-GROUP = 4
+GROUP = 6
 CHUNK = 64
 
 
@@ -258,8 +258,9 @@
     slots, blocks, offsets_from, high_ref, low_ref, weights_ref, right_a, right_b, one_ref, *refs
 ):
     columns, refs = refs[: 2 * slots - 1], refs[2 * slots - 1 :]
-    right_refs, refs = refs[:-9], refs[-9:]
-    out_ref, right_ref, total, prediction, turned, sums, offsets_ref, arrived, left_ref = refs
+    right_refs, refs = refs[:-10], refs[-10:]
+    ends_ref, out_ref, right_ref, total, prediction, turned, sums, offsets_ref, arrived = refs[:9]
+    left_ref = refs[9]
     copy = pltpu.make_async_copy(offsets_from, offsets_ref, arrived)
     copy.start()
     row, column, same = position(slots, blocks)
@@ -290,8 +291,10 @@
     to_traces(prediction, total, (high_ref[...], low_ref[...]))
     copy.wait()
     added = matched(prediction, weights_ref, offsets_ref, turned, sums)
-    for receiver in range(receivers):
-        out_ref[receiver] = added[receiver]
+    ends_ref[0] = added[0]
+    ends_ref[1] = added[-1]
+    for receiver in range(1, receivers - 1):
+        out_ref[receiver - 1] = added[receiver]
 
 
 def mirror_kernel(
@@ -320,15 +323,12 @@
     to_traces(prediction, total, tables)
     copy.wait()
     added = matched_halo(prediction[...], weights_ref, offsets_ref, turned)
-    last = out_ref.shape[0] - 1
-    out_ref[...] = part_ref[...]
-    out_ref[0] = out_ref[0] + added[0]
-    out_ref[last] = out_ref[last] + added[1]
+    out_ref[...] = part_ref[...] + added
 
 
 def own_kernel(
     slots, blocks, offsets_from, high_ref, low_ref, weights_ref, right_ref, halo_ref,
-    recorded_ref, here_ref, one_ref, *refs
+    recorded_ref, inner_ref, here_ref, one_ref, *refs
 ):
     columns, refs = refs[: 2 * slots - 2], refs[2 * slots - 2 :]
     out_ref, total, prediction, turned, sums, offsets_ref, arrived, left_ref = refs
@@ -361,11 +361,16 @@
             value = value - outer[0]
         if receiver == last:
             value = value - outer[1]
+        if 0 < receiver < last:
+            value = value - inner_ref[receiver - 1]
         out_ref[receiver] = value
 
 
-def last_kernel(part_ref, arrived_ref, out_ref):
-    out_ref[...] = part_ref[...] - arrived_ref[...]
+def last_kernel(part_ref, ends_ref, out_ref):
+    last = out_ref.shape[0] - 1
+    out_ref[...] = part_ref[...]
+    out_ref[0] = part_ref[0] - ends_ref[0]
+    out_ref[last] = part_ref[last] - ends_ref[1]
 
 
 def call(kernel, arrays, outs, scratch, in_place=0):
@@ -471,30 +476,32 @@
     for k in range(1, slots):
         ones_twos += gathered[3 * k - 1 : 3 * k + 1]
         heres_ones += gathered[3 * k - 2 : 3 * k]
-    part, right = call(
+    ends_shape = (2, sources, samples)
+    ends, inner, right = call(
         functools.partial(main_kernel, slots, blocks),
         [offsets, high, low, mirror_weights, right_a, right_b, one_spectra] + ones_twos + rest,
-        [recorded.shape, right_shape],
+        [ends_shape, (receivers - 2, sources, samples), right_shape],
         scratch_of(receivers) + sums + taken + [own_shape],
         in_place=1,
     )
-    mirror_part, halo = call(
+    inner = permute(inner, lambda i, j: (i ^ blocks, j))
+    ends, halo = call(
         functools.partial(mirror_kernel, blocks),
-        [offsets, high, low, mirror_weights, near, far, part, right],
-        [recorded.shape, (4, held, width + samples)],
+        [offsets, high, low, mirror_weights, near, far, ends, right],
+        [ends_shape, (4, held, width + samples)],
         scratch_of(2) + taken + [(4, held, samples)],
         in_place=1,
     )
-    arrived = permute(mirror_part, lambda i, j: (i ^ blocks, j))
+    ends = permute(ends, lambda i, j: (i ^ blocks, j))
     (own_part,) = call(
         functools.partial(own_kernel, slots, blocks),
-        [offsets, high, low, weights, right, halo, recorded, here_spectra, one_spectra]
+        [offsets, high, low, weights, right, halo, recorded, inner, here_spectra, one_spectra]
         + heres_ones,
         [recorded.shape],
         scratch_of(receivers + 2) + sums + taken + [own_shape],
         in_place=1,
     )
-    (out,) = call(last_kernel, [own_part, arrived], [recorded.shape], [])
+    (out,) = call(last_kernel, [own_part, ends], [recorded.shape], [])
     return out
 
 

time: 42.8 us -> 42.1 us (0.984)
  waiting for transfers between devices: 8.54 us -> 6.17 us
  starting transfers between devices: 16 us -> 18 us
    ppermute x13 -> x14, waiting for transfers between devices: 8.54 us -> 6.17 us  [permute(): return lax.ppermute(array, AXES, pairs)]
    ppermute x13 -> x14, starting transfers between devices: 16 us -> 18 us  [permute(): return lax.ppermute(array, AXES, pairs)]
  transfers between devices with their start and end apart: 13 -> 14, of which waited for: 5 -> 3; matrix products, arithmetic and copies ran while one was open for 0% -> 0% of each run, Pallas kernels for 26% -> 31%
where the time goes in v2:
time: 42.1 us; the launch traced here: 41.9 us
  starting transfers between devices  18 us (43%)
  Pallas kernels  13.8 us (33%)
  waiting for transfers between devices  6.17 us (15%)
  local copies, waits for them, and re-layouts  3.73 us (9%)
    ppermute x14, starting transfers between devices, permute(): return lax.ppermute(array, AXES, pairs)  18 us
    pallas_call x7, Pallas kernels, call(): pl.pallas_call(kernel, out_shape=shapes, in_specs=[pl.BlockSpec(memory_sp...  13.8 us
    ppermute x14, waiting for transfers between devices, permute(): return lax.ppermute(array, AXES, pairs)  6.17 us
    unnamed x12, local copies, waits for them, and re-layouts  3.71 us
  transfers between devices with their start and end apart: 14, of which 3 were waited for; matrix products, arithmetic and copies ran while one was open for 0% of the time, Pallas kernels for 31%

profile of v2, /device:TPU:0, one launch (start us, length us, event | category | flops | bytes accessed | tf_op | source)
XLA Modules:
  0.0 41.9 jit_solution(3705891839049883123)
XLA Ops:
  0.0 3.0 %collective-permute-start.1 = (f32[8,16,512]{2,1,0:T(8,128)}, f32[8,16,512]{2,1,0:T(8,128)S(1)}, u32[]{:S(2)}, u32[]{:S(2)}) collective-permute-start(f32[8,16,512]{2,1,0:T(8,128)} %right_ref.1), channel_id=1, source_target_pairs={{0,4},{1,5},{2,6},{3,7},{4,0},{5,1},{6,2},{7,3},{8,12},{9,13},{10,... | collective-permute-start | bytes 786440 | tf_op jit(solution)/shard_map/ppermute | solution.py:403
  3.0 1.6 %collective-permute-start.2 = (f32[8,16,512]{2,1,0:T(8,128)}, f32[8,16,512]{2,1,0:T(8,128)S(1)}, u32[]{:S(2)}, u32[]{:S(2)}) collective-permute-start(f32[8,16,512]{2,1,0:T(8,128)} %right_ref.1), channel_id=1, source_target_pairs={{0,8},{1,9},{2,10},{3,11},{4,12},{5,13},{6,14},{7,15},{8,0},{9,1},... | collective-permute-start | bytes 786440 | tf_op jit(solution)/shard_map/ppermute | solution.py:403
  4.5 1.5 %collective-permute-start = (f32[4,16,512]{2,1,0:T(8,128)}, f32[4,16,512]{2,1,0:T(8,128)S(1)}, u32[]{:S(2)}, u32[]{:S(2)}) collective-permute-start(f32[4,16,512]{2,1,0:T(8,128)} %refs_0_.1), channel_id=1, source_target_pairs={{0,2},{1,3},{2,18},{3,19},{4,6},{5,7},{6,22},{7,23},{8,10},{9,11},... | collective-permute-start | bytes 393224 | tf_op jit(solution)/shard_map/ppermute | solution.py:403
  6.0 0.9 %copy-done = f32[4,16,512]{2,1,0:T(8,128)S(1)} copy-done((f32[4,16,512]{2,1,0:T(8,128)S(1)}, f32[4,16,512]{2,1,0:T(8,128)}, u32[]{:S(2)}) %copy-start) | copy-done | bytes 131096
  7.0 0.9 %copy-done.1 = f32[8,16,512]{2,1,0:T(8,128)S(1)} copy-done((f32[8,16,512]{2,1,0:T(8,128)S(1)}, f32[8,16,512]{2,1,0:T(8,128)}, u32[]{:S(2)}) %copy-start.1) | copy-done | bytes 262168
  7.9 0.9 %copy-done.2 = f32[96,512]{1,0:T(8,128)S(1)} copy-done((f32[96,512]{1,0:T(8,128)S(1)}, f32[96,512]{1,0:T(8,128)}, u32[]{:S(2)}) %copy-start.2) | copy-done | bytes 196632
  8.9 0.9 %copy-done.4 = f32[3,21,4,16]{1,3,2,0:T(8,128)S(1)} copy-done((f32[3,21,4,16]{1,3,2,0:T(8,128)S(1)}, f32[3,21,4,16]{1,3,2,0:T(8,128)}, u32[]{:S(2)}) %copy-start.4) | copy-done | bytes 16152
  9.7 1.2 %shard_map.64 = (bf16[512,1024]{1,0:T(8,128)(2,1)S(1)}, bf16[512,1024]{1,0:T(8,128)(2,1)S(1)}, f32[88,128]{1,0:T(8,128)S(1)}, f32[4,16,1536]{2,1,0:T(8,128)S(1)}, f32[8,16,1024]{2,1,0:T(8,128)S(1)}) custom-call(f32[96,512]{1,0:T(8,128)S(1)} %copy-done.2, f32[3,4,16,21]{3,2,1,0:T(8,128)S(1)} %bitcast.1, f32[4,16,512]{2,1,0:T(8,128)S(1)} %copy-done, ...), custom_call_target="tpu_custom_call" | custom-call | tf_op jit(solution)/shard_map/pallas_call | solution.py:379
  11.0 2.8 %collective-permute-done.2.refs_1_ = f32[8,16,512]{2,1,0:T(8,128)S(1)} collective-permute-done((f32[8,16,512]{2,1,0:T(8,128)}, f32[8,16,512]{2,1,0:T(8,128)S(1)}, u32[]{:S(2)}, u32[]{:S(2)}) %collective-permute-start.2) | collective-permute-done | bytes 262176 | tf_op jit(solution)/shard_map/ppermute | solution.py:403
  13.8 2.6 %collective-permute-start.4 = (f32[4,16,512]{2,1,0:T(8,128)S(1)}, f32[4,16,512]{2,1,0:T(8,128)S(1)}, u32[]{:S(2)}, u32[]{:S(2)}) collective-permute-start(f32[4,16,512]{2,1,0:T(8,128)S(1)} %collective-permute-done.one_ref.refs_1_), channel_id=1, source_target_pairs={{0,2},{1,3},{4,6},{5,7},{8,10},{9,11},{12,14},{13,15},{18,16},{19,... | collective-permute-start | bytes 393224 | tf_op jit(solution)/shard_map/ppermute | solution.py:403
  16.6 0.6 %collective-permute-start.8 = (f32[4,16,512]{2,1,0:T(8,128)S(1)}, f32[4,16,512]{2,1,0:T(8,128)S(1)}, u32[]{:S(2)}, u32[]{:S(2)}) collective-permute-start(f32[4,16,512]{2,1,0:T(8,128)S(1)} %slice.6), channel_id=1, source_target_pairs={{0,4},{1,5},{2,6},{3,7},{4,0},{5,1},{6,2},{7,3},{8,12},{9,13},{10,... | collective-permute-start | bytes 393224 | tf_op jit(solution)/shard_map/ppermute | solution.py:403
  17.1 1.3 %collective-permute-start.9 = (f32[4,16,512]{2,1,0:T(8,128)S(1)}, f32[4,16,512]{2,1,0:T(8,128)S(1)}, u32[]{:S(2)}, u32[]{:S(2)}) collective-permute-start(f32[4,16,512]{2,1,0:T(8,128)S(1)} %slice.7), channel_id=1, source_target_pairs={{0,8},{1,9},{2,10},{3,11},{4,12},{5,13},{6,14},{7,15},{8,0},{9,1},... | collective-permute-start | bytes 393224 | tf_op jit(solution)/shard_map/ppermute | solution.py:403
  18.5 1.2 %shard_map.65 = (f32[4,16,1536]{2,1,0:T(8,128)S(1)}, f32[16,16,1024]{2,1,0:T(8,128)S(1)}) custom-call(bf16[512,1024]{1,0:T(8,128)(2,1)S(1)} %get-tuple-element.44.high_ref, bf16[512,1024]{1,0:T(8,128)(2,1)S(1)} %get-tuple-element.45.low_ref, f32[4,16,512]{2,1,0:T(8,128)S(1)} %collective-permute-done.one_ref.refs_1_, ...), custom_call_target="tpu_custom_call" | custom-call | tf_op jit(solution)/shard_map/pallas_call | solution.py:379
  19.7 2.9 %collective-permute-done.6.weights_ref = f32[88,128]{1,0:T(8,128)S(1)} collective-permute-done((f32[88,128]{1,0:T(8,128)S(1)}, f32[88,128]{1,0:T(8,128)S(1)}, u32[]{:S(2)}, u32[]{:S(2)}) %collective-permute-start.6) | collective-permute-done | bytes 45088 | tf_op jit(solution)/shard_map/ppermute | solution.py:403
  22.5 0.7 %collective-permute-start.7 = (f32[4,16,512]{2,1,0:T(8,128)S(1)}, f32[4,16,512]{2,1,0:T(8,128)S(1)}, u32[]{:S(2)}, u32[]{:S(2)}) collective-permute-start(f32[4,16,512]{2,1,0:T(8,128)S(1)} %collective-permute-done.4.refs_0_.refs_2_), channel_id=1, source_target_pairs={{2,3},{3,2},{6,7},{7,6},{10,11},{11,10},{14,15},{15,14},{16,17},{1... | collective-permute-start | bytes 393224 | tf_op jit(solution)/shard_map/ppermute | solution.py:403
  23.2 0.5 %collective-permute-done.9.refs_4_ = f32[4,16,512]{2,1,0:T(8,128)S(1)} collective-permute-done((f32[4,16,512]{2,1,0:T(8,128)S(1)}, f32[4,16,512]{2,1,0:T(8,128)S(1)}, u32[]{:S(2)}, u32[]{:S(2)}) %collective-permute-start.9) | collective-permute-done | bytes 131104 | tf_op jit(solution)/shard_map/ppermute | solution.py:403
  23.8 1.1 %collective-permute-start.10 = (f32[2,32,512]{2,1,0:T(8,128)S(1)}, f32[2,32,512]{2,1,0:T(8,128)S(1)}, u32[]{:S(2)}, u32[]{:S(2)}) collective-permute-start(f32[2,32,512]{2,1,0:T(8,128)S(1)} %get-tuple-element.66), channel_id=1, source_target_pairs={{0,4},{1,5},{2,6},{3,7},{4,0},{5,1},{6,2},{7,3},{8,12},{9,13},{10,... | collective-permute-start | bytes 393224 | tf_op jit(solution)/shard_map/ppermute | solution.py:403
  24.9 0.7 %collective-permute-start.11 = (f32[2,32,512]{2,1,0:T(8,128)S(1)}, f32[2,32,512]{2,1,0:T(8,128)S(1)}, u32[]{:S(2)}, u32[]{:S(2)}) collective-permute-start(f32[2,32,512]{2,1,0:T(8,128)S(1)} %get-tuple-element.67), channel_id=1, source_target_pairs={{0,12},{1,13},{2,14},{3,15},{4,8},{5,9},{6,10},{7,11},{8,4},{9,5},... | collective-permute-start | bytes 393224 | tf_op jit(solution)/shard_map/ppermute | solution.py:403
  25.6 3.9 %shard_map.66 = (f32[2,16,512]{2,1,0:T(8,128)S(1)}, f32[2,16,512]{2,1,0:T(8,128)S(1)}, f32[32,16,1024]{2,1,0:T(8,128)S(1)}) custom-call(s32[21]{0:T(128)S(1)} %copy-done.5, bf16[512,1024]{1,0:T(8,128)(2,1)S(1)} %get-tuple-element.44.high_ref, bf16[512,1024]{1,0:T(8,128)(2,1)S(1)} %get-tuple-element.45.low_ref, ...), custom_call_target="tpu_custom_call" | custom-call | tf_op jit(solution)/shard_map/pallas_call | solution.py:379
  29.6 3.2 %collective-permute-start.12 = (f32[2,16,512]{2,1,0:T(8,128)S(1)}, f32[2,16,512]{2,1,0:T(8,128)S(1)}, u32[]{:S(2)}, u32[]{:S(2)}) collective-permute-start(f32[2,16,512]{2,1,0:T(8,128)S(1)} %get-tuple-element.70), channel_id=1, source_target_pairs={{0,16},{1,17},{2,18},{3,19},{4,20},{5,21},{6,22},{7,23},{8,24},{9,... | collective-permute-start | bytes 196616 | tf_op jit(solution)/shard_map/ppermute | solution.py:403
  32.8 2.3 %shard_map.68 = (f32[2,16,512]{2,1,0:T(8,128)S(1)}, f32[4,32,1536]{2,1,0:T(8,128)S(1)}) custom-call(s32[21]{0:T(128)S(1)} %copy-done.5, bf16[512,1024]{1,0:T(8,128)(2,1)S(1)} %get-tuple-element.44.high_ref, bf16[512,1024]{1,0:T(8,128)(2,1)S(1)} %get-tuple-element.45.low_ref, f32[88,128]{1,0:T(8,128)S(1)} %collective-permute-done.6.weights_ref, ...), custom_call_target="tpu_custom_call" | custom-call | tf_op jit(solution)/shard_map/pallas_call | solution.py:379
  35.1 1.6 %collective-permute-start.13 = (f32[2,16,512]{2,1,0:T(8,128)S(1)}, f32[2,16,512]{2,1,0:T(8,128)S(1)}, u32[]{:S(2)}, u32[]{:S(2)}) collective-permute-start(f32[2,16,512]{2,1,0:T(8,128)S(1)} %get-tuple-element.72), channel_id=1, source_target_pairs={{0,16},{1,17},{2,18},{3,19},{4,20},{5,21},{6,22},{7,23},{8,24},{9,... | collective-permute-start | bytes 196616 | tf_op jit(solution)/shard_map/ppermute | solution.py:403
  36.7 4.4 %shard_map.69.part_ref = f32[4,16,512]{2,1,0:T(8,128)S(1)} custom-call(s32[21]{0:T(128)S(1)} %copy-done.5, bf16[512,1024]{1,0:T(8,128)(2,1)S(1)} %get-tuple-element.44.high_ref, bf16[512,1024]{1,0:T(8,128)(2,1)S(1)} %get-tuple-element.45.low_ref, f32[88,128]{1,0:T(8,128)S(1)} %get-tuple-element.46.weights_ref, ...), custom_call_target="tpu_custom_call" | custom-call | tf_op jit(solution)/shard_map/pallas_call | solution.py:379
  41.2 0.7 %shard_map.70 = f32[4,16,512]{2,1,0:T(8,128)} custom-call(f32[4,16,512]{2,1,0:T(8,128)S(1)} %shard_map.69.part_ref, f32[2,16,512]{2,1,0:T(8,128)S(1)} %collective-permute-done.13.ends_ref), custom_call_target="tpu_custom_call" | custom-call | tf_op jit(solution)/shard_map/pallas_call | solution.py:379
  (25 shorter events, 0.3 us)
Async XLA Ops:
  0.0 11.0 %collective-permute-start.1 = (f32[8,16,512]{2,1,0:T(8,128)}, f32[8,16,512]{2,1,0:T(8,128)S(1)}, u32[]{:S(2)}, u32[]{:S(2)}) collective-permute-start(f32[8,16,512]{2,1,0:T(8,128)} %right_ref.1), channel_id=1, source_target_pairs={{0,4},{1,5},{2,6},{3,7},{4,0},{5,1},{6,2},{7,3},{8,12},{9,13},{10,... | collective-permute-start | bytes 786440 | tf_op jit(solution)/shard_map/ppermute | solution.py:403
  3.0 10.8 %collective-permute-start.2 = (f32[8,16,512]{2,1,0:T(8,128)}, f32[8,16,512]{2,1,0:T(8,128)S(1)}, u32[]{:S(2)}, u32[]{:S(2)}) collective-permute-start(f32[8,16,512]{2,1,0:T(8,128)} %right_ref.1), channel_id=1, source_target_pairs={{0,8},{1,9},{2,10},{3,11},{4,12},{5,13},{6,14},{7,15},{8,0},{9,1},... | collective-permute-start | bytes 786440 | tf_op jit(solution)/shard_map/ppermute | solution.py:403
  4.5 6.4 %collective-permute-start = (f32[4,16,512]{2,1,0:T(8,128)}, f32[4,16,512]{2,1,0:T(8,128)S(1)}, u32[]{:S(2)}, u32[]{:S(2)}) collective-permute-start(f32[4,16,512]{2,1,0:T(8,128)} %refs_0_.1), channel_id=1, source_target_pairs={{0,2},{1,3},{2,18},{3,19},{4,6},{5,7},{6,22},{7,23},{8,10},{9,11},... | collective-permute-start | bytes 393224 | tf_op jit(solution)/shard_map/ppermute | solution.py:403
  6.0 4.9 %collective-permute-start.3 = (f32[4,16,512]{2,1,0:T(8,128)}, f32[4,16,512]{2,1,0:T(8,128)S(1)}, u32[]{:S(2)}, u32[]{:S(2)}) collective-permute-start(f32[4,16,512]{2,1,0:T(8,128)} %refs_0_.1), channel_id=1, source_target_pairs={{0,1},{1,0},{2,3},{3,2},{4,5},{5,4},{6,7},{7,6},{8,9},{9,8},{10,11... | collective-permute-start | bytes 393224 | tf_op jit(solution)/shard_map/ppermute | solution.py:403
  6.0 0.9 %copy-start = (f32[4,16,512]{2,1,0:T(8,128)S(1)}, f32[4,16,512]{2,1,0:T(8,128)}, u32[]{:S(2)}) copy-start(f32[4,16,512]{2,1,0:T(8,128)} %refs_0_.1) | copy-start | bytes 393220
  7.0 0.9 %copy-start.1 = (f32[8,16,512]{2,1,0:T(8,128)S(1)}, f32[8,16,512]{2,1,0:T(8,128)}, u32[]{:S(2)}) copy-start(f32[8,16,512]{2,1,0:T(8,128)} %right_ref.1) | copy-start | bytes 786436
  7.9 0.9 %copy-start.2 = (f32[96,512]{1,0:T(8,128)S(1)}, f32[96,512]{1,0:T(8,128)}, u32[]{:S(2)}) copy-start(f32[96,512]{1,0:T(8,128)} %constant.2.clone.phases_ref) | copy-start | bytes 589828
  8.9 0.9 %copy-start.4 = (f32[3,21,4,16]{1,3,2,0:T(8,128)S(1)}, f32[3,21,4,16]{1,3,2,0:T(8,128)}, u32[]{:S(2)}) copy-start(f32[3,21,4,16]{1,3,2,0:T(8,128)} %param.9) | copy-start | bytes 48388
  10.9 14.7 %copy-start.5 = (s32[21]{0:T(128)S(1)}, s32[21]{0:T(128)}, u32[]{:S(2)}) copy-start(s32[21]{0:T(128)} %offsets_from.5) | copy-start | bytes 256
  13.8 8.8 %collective-permute-start.4 = (f32[4,16,512]{2,1,0:T(8,128)S(1)}, f32[4,16,512]{2,1,0:T(8,128)S(1)}, u32[]{:S(2)}, u32[]{:S(2)}) collective-permute-start(f32[4,16,512]{2,1,0:T(8,128)S(1)} %collective-permute-done.one_ref.refs_1_), channel_id=1, source_target_pairs={{0,2},{1,3},{4,6},{5,7},{8,10},{9,11},{12,14},{13,15},{18,16},{19,... | collective-permute-start | bytes 393224 | tf_op jit(solution)/shard_map/ppermute | solution.py:403
  16.4 6.2 %collective-permute-start.5 = (f32[4,16,512]{2,1,0:T(8,128)S(1)}, f32[4,16,512]{2,1,0:T(8,128)S(1)}, u32[]{:S(2)}, u32[]{:S(2)}) collective-permute-start(f32[4,16,512]{2,1,0:T(8,128)S(1)} %collective-permute-done.one_ref.refs_1_), channel_id=1, source_target_pairs={{0,1},{1,0},{2,3},{3,2},{4,5},{5,4},{6,7},{7,6},{8,9},{9,8},{10,11... | collective-permute-start | bytes 393224 | tf_op jit(solution)/shard_map/ppermute | solution.py:403
  16.5 6.1 %collective-permute-start.6 = (f32[88,128]{1,0:T(8,128)S(1)}, f32[88,128]{1,0:T(8,128)S(1)}, u32[]{:S(2)}, u32[]{:S(2)}) collective-permute-start(f32[88,128]{1,0:T(8,128)S(1)} %get-tuple-element.46.weights_ref), channel_id=1, source_target_pairs={{0,16},{1,17},{2,18},{3,19},{4,20},{5,21},{6,22},{7,23},{8,24},{9,... | collective-permute-start | bytes 135176 | tf_op jit(solution)/shard_map/ppermute | solution.py:403
  16.6 6.7 %collective-permute-start.8 = (f32[4,16,512]{2,1,0:T(8,128)S(1)}, f32[4,16,512]{2,1,0:T(8,128)S(1)}, u32[]{:S(2)}, u32[]{:S(2)}) collective-permute-start(f32[4,16,512]{2,1,0:T(8,128)S(1)} %slice.6), channel_id=1, source_target_pairs={{0,4},{1,5},{2,6},{3,7},{4,0},{5,1},{6,2},{7,3},{8,12},{9,13},{10,... | collective-permute-start | bytes 393224 | tf_op jit(solution)/shard_map/ppermute | solution.py:403
  17.1 6.6 %collective-permute-start.9 = (f32[4,16,512]{2,1,0:T(8,128)S(1)}, f32[4,16,512]{2,1,0:T(8,128)S(1)}, u32[]{:S(2)}, u32[]{:S(2)}) collective-permute-start(f32[4,16,512]{2,1,0:T(8,128)S(1)} %slice.7), channel_id=1, source_target_pairs={{0,8},{1,9},{2,10},{3,11},{4,12},{5,13},{6,14},{7,15},{8,0},{9,1},... | collective-permute-start | bytes 393224 | tf_op jit(solution)/shard_map/ppermute | solution.py:403
  22.5 1.2 %collective-permute-start.7 = (f32[4,16,512]{2,1,0:T(8,128)S(1)}, f32[4,16,512]{2,1,0:T(8,128)S(1)}, u32[]{:S(2)}, u32[]{:S(2)}) collective-permute-start(f32[4,16,512]{2,1,0:T(8,128)S(1)} %collective-permute-done.4.refs_0_.refs_2_), channel_id=1, source_target_pairs={{2,3},{3,2},{6,7},{7,6},{10,11},{11,10},{14,15},{15,14},{16,17},{1... | collective-permute-start | bytes 393224 | tf_op jit(solution)/shard_map/ppermute | solution.py:403
  23.8 9.0 %collective-permute-start.10 = (f32[2,32,512]{2,1,0:T(8,128)S(1)}, f32[2,32,512]{2,1,0:T(8,128)S(1)}, u32[]{:S(2)}, u32[]{:S(2)}) collective-permute-start(f32[2,32,512]{2,1,0:T(8,128)S(1)} %get-tuple-element.66), channel_id=1, source_target_pairs={{0,4},{1,5},{2,6},{3,7},{4,0},{5,1},{6,2},{7,3},{8,12},{9,13},{10,... | collective-permute-start | bytes 393224 | tf_op jit(solution)/shard_map/ppermute | solution.py:403
  24.9 7.9 %collective-permute-start.11 = (f32[2,32,512]{2,1,0:T(8,128)S(1)}, f32[2,32,512]{2,1,0:T(8,128)S(1)}, u32[]{:S(2)}, u32[]{:S(2)}) collective-permute-start(f32[2,32,512]{2,1,0:T(8,128)S(1)} %get-tuple-element.67), channel_id=1, source_target_pairs={{0,12},{1,13},{2,14},{3,15},{4,8},{5,9},{6,10},{7,11},{8,4},{9,5},... | collective-permute-start | bytes 393224 | tf_op jit(solution)/shard_map/ppermute | solution.py:403
  29.6 7.2 %collective-permute-start.12 = (f32[2,16,512]{2,1,0:T(8,128)S(1)}, f32[2,16,512]{2,1,0:T(8,128)S(1)}, u32[]{:S(2)}, u32[]{:S(2)}) collective-permute-start(f32[2,16,512]{2,1,0:T(8,128)S(1)} %get-tuple-element.70), channel_id=1, source_target_pairs={{0,16},{1,17},{2,18},{3,19},{4,20},{5,21},{6,22},{7,23},{8,24},{9,... | collective-permute-start | bytes 196616 | tf_op jit(solution)/shard_map/ppermute | solution.py:403
  32.8 4.0 %copy-start.3 = (f32[4,16,512]{2,1,0:T(8,128)S(1)}, f32[4,16,512]{2,1,0:T(8,128)}, u32[]{:S(2)}) copy-start(f32[4,16,512]{2,1,0:T(8,128)} %recorded_ref.1) | copy-start | bytes 393220
  35.1 6.1 %collective-permute-start.13 = (f32[2,16,512]{2,1,0:T(8,128)S(1)}, f32[2,16,512]{2,1,0:T(8,128)S(1)}, u32[]{:S(2)}, u32[]{:S(2)}) collective-permute-start(f32[2,16,512]{2,1,0:T(8,128)S(1)} %get-tuple-element.72), channel_id=1, source_target_pairs={{0,16},{1,17},{2,18},{3,19},{4,20},{5,21},{6,22},{7,23},{8,24},{9,... | collective-permute-start | bytes 196616 | tf_op jit(solution)/shard_map/ppermute | solution.py:403

commit v3 on v2

--- a/solution.py
+++ b/solution.py
@@ -83,6 +83,12 @@
     return jnp.concatenate([values, total], axis=-1)
 
 
+def with_differences(values):
+    half = values.shape[-1] // 2
+    real, imag = values[..., :half], values[..., half:]
+    return jnp.concatenate([real, imag - real, imag + real], axis=-1)
+
+
 def products(total_ref, lefts, right_ref):
     _, sources, width = total_ref.shape
     half = width // 2
@@ -97,9 +103,8 @@
             for bounce in range(right_ref.shape[0]):
                 at = slice(bounce, bounce + 1)
                 right_real = right_ref[bounce, :, real]
-                right_imag = right_ref[bounce, :, imag]
-                right_more = right_imag - right_real
-                right_both = right_imag + right_real
+                right_more = right_ref[bounce, :, imag]
+                right_both = right_ref[bounce, :, both]
                 for index, (_, left_ref, row) in enumerate(members):
                     one, two, three = sums[index]
                     sums[index] = (
@@ -277,7 +282,7 @@
         step = min(count, value.shape[0])
         for first in range(0, value.shape[0], step):
             at = jnp.bitwise_xor(row, place // count) % blocks * count + place % count
-            right_ref[pl.ds(at, step)] = value[first : first + step]
+            right_ref[pl.ds(at, step)] = with_differences(value[first : first + step])
             place += step
     receivers, held, _ = one_ref.shape
     for slot in range(slots):
@@ -411,7 +416,7 @@
     one = permute(
         rb_data, lambda i, j: (i, j ^ slots) if is_same(i, j) else (i ^ blocks, j)
     )
-    some = [permute(bs_data, lambda i, j, k=k: (i ^ k, j)) for k in range(1, cut)]
+    some = [permute(bs_data, lambda i, j, k=k: (i ^ k, j)) for k in range(cut - 1, 0, -1)]
     heres = [rb_data] + [
         permute(rb_data, lambda i, j, k=k: (i, j ^ k)) for k in range(1, slots)
     ]
@@ -429,6 +434,7 @@
     one, some, heres, high, low, weights, here_spectra, right_a = lax.optimization_barrier(
         (one, some, heres, high, low, weights, here_spectra, right_a)
     )
+    some = some[::-1]
     two = permute(one, lambda i, j: (i, j ^ slots) if is_same(i, j) else None)
     ones = [permute(one, lambda i, j, k=k: (i, j ^ k)) for k in range(1, slots)]
     rest = []
@@ -463,7 +469,7 @@
     near = permute(near, lambda i, j: (i ^ 1, j))
     far = permute(far, lambda i, j: (in_half(i, i + 1 if i % 2 else i - 1), j))
     per = samples * receivers * sources // LANES
-    right_shape = (blocks * right_count, sources, width)
+    right_shape = (blocks * right_count, sources, width + samples)
     own_shape = (receivers, held, width + samples)
 
     def scratch_of(predicted):

time: 42.1 us -> 41.8 us (level)
  waiting for transfers between devices: 6.17 us -> 4.62 us
  starting transfers between devices: 18 us -> 19.3 us
    ppermute x14, waiting for transfers between devices: 6.17 us -> 4.62 us  [permute(): return lax.ppermute(array, AXES, pairs)]
    ppermute x14, starting transfers between devices: 18 us -> 19.3 us  [permute(): return lax.ppermute(array, AXES, pairs)]
    unnamed x12 -> x14, local copies, waits for them, and re-layouts: 3.71 us -> 3.72 us
  transfers between devices with their start and end apart: 14 -> 14, of which waited for: 3 -> 3; matrix products, arithmetic and copies ran while one was open for 0% -> 0% of each run, Pallas kernels for 31% -> 32%
where the time goes in v3:
time: 41.8 us; the launch traced here: 41.6 us
  starting transfers between devices  19.3 us (46%)
  Pallas kernels  13.8 us (33%)
  waiting for transfers between devices  4.62 us (11%)
  local copies, waits for them, and re-layouts  3.73 us (9%)
    ppermute x14, starting transfers between devices, permute(): return lax.ppermute(array, AXES, pairs)  19.3 us
    pallas_call x7, Pallas kernels, call(): pl.pallas_call(kernel, out_shape=shapes, in_specs=[pl.BlockSpec(memory_sp...  13.8 us
    ppermute x14, waiting for transfers between devices, permute(): return lax.ppermute(array, AXES, pairs)  4.62 us
    unnamed x14, local copies, waits for them, and re-layouts  3.72 us
  transfers between devices with their start and end apart: 14, of which 3 were waited for; matrix products, arithmetic and copies ran while one was open for 0% of the time, Pallas kernels for 32%

profile of v3, /device:TPU:0, one launch (start us, length us, event | category | flops | bytes accessed | tf_op | source)
XLA Modules:
  0.0 41.6 jit_solution(15670220197425330344)
XLA Ops:
  0.0 3.0 %collective-permute-start.1 = (f32[8,16,512]{2,1,0:T(8,128)}, f32[8,16,512]{2,1,0:T(8,128)S(1)}, u32[]{:S(2)}, u32[]{:S(2)}) collective-permute-start(f32[8,16,512]{2,1,0:T(8,128)} %right_ref.1), channel_id=1, source_target_pairs={{0,8},{1,9},{2,10},{3,11},{4,12},{5,13},{6,14},{7,15},{8,0},{9,1},... | collective-permute-start | bytes 786440 | tf_op jit(solution)/shard_map/ppermute | solution.py:408
  3.0 1.5 %collective-permute-start.2 = (f32[8,16,512]{2,1,0:T(8,128)}, f32[8,16,512]{2,1,0:T(8,128)S(1)}, u32[]{:S(2)}, u32[]{:S(2)}) collective-permute-start(f32[8,16,512]{2,1,0:T(8,128)} %right_ref.1), channel_id=1, source_target_pairs={{0,4},{1,5},{2,6},{3,7},{4,0},{5,1},{6,2},{7,3},{8,12},{9,13},{10,... | collective-permute-start | bytes 786440 | tf_op jit(solution)/shard_map/ppermute | solution.py:408
  4.5 1.5 %collective-permute-start = (f32[4,16,512]{2,1,0:T(8,128)}, f32[4,16,512]{2,1,0:T(8,128)S(1)}, u32[]{:S(2)}, u32[]{:S(2)}) collective-permute-start(f32[4,16,512]{2,1,0:T(8,128)} %refs_0_.1), channel_id=1, source_target_pairs={{0,2},{1,3},{2,18},{3,19},{4,6},{5,7},{6,22},{7,23},{8,10},{9,11},... | collective-permute-start | bytes 393224 | tf_op jit(solution)/shard_map/ppermute | solution.py:408
  6.0 0.9 %copy-done = f32[4,16,512]{2,1,0:T(8,128)S(1)} copy-done((f32[4,16,512]{2,1,0:T(8,128)S(1)}, f32[4,16,512]{2,1,0:T(8,128)}, u32[]{:S(2)}) %copy-start) | copy-done | bytes 131096
  7.0 0.9 %copy-done.2 = f32[8,16,512]{2,1,0:T(8,128)S(1)} copy-done((f32[8,16,512]{2,1,0:T(8,128)S(1)}, f32[8,16,512]{2,1,0:T(8,128)}, u32[]{:S(2)}) %copy-start.2) | copy-done | bytes 262168
  7.9 0.9 %copy-done.3 = f32[96,512]{1,0:T(8,128)S(1)} copy-done((f32[96,512]{1,0:T(8,128)S(1)}, f32[96,512]{1,0:T(8,128)}, u32[]{:S(2)}) %copy-start.3) | copy-done | bytes 196632
  8.9 0.9 %copy-done.5 = f32[3,21,4,16]{1,3,2,0:T(8,128)S(1)} copy-done((f32[3,21,4,16]{1,3,2,0:T(8,128)S(1)}, f32[3,21,4,16]{1,3,2,0:T(8,128)}, u32[]{:S(2)}) %copy-start.5) | copy-done | bytes 16152
  9.8 1.2 %shard_map.64 = (bf16[512,1024]{1,0:T(8,128)(2,1)S(1)}, bf16[512,1024]{1,0:T(8,128)(2,1)S(1)}, f32[88,128]{1,0:T(8,128)S(1)}, f32[4,16,1536]{2,1,0:T(8,128)S(1)}, f32[8,16,1024]{2,1,0:T(8,128)S(1)}) custom-call(f32[96,512]{1,0:T(8,128)S(1)} %copy-done.3, f32[3,4,16,21]{3,2,1,0:T(8,128)S(1)} %bitcast.1, f32[4,16,512]{2,1,0:T(8,128)S(1)} %copy-done, ...), custom_call_target="tpu_custom_call" | custom-call | tf_op jit(solution)/shard_map/pallas_call | solution.py:384
  11.0 1.4 %collective-permute-done.1.refs_1_ = f32[8,16,512]{2,1,0:T(8,128)S(1)} collective-permute-done((f32[8,16,512]{2,1,0:T(8,128)}, f32[8,16,512]{2,1,0:T(8,128)S(1)}, u32[]{:S(2)}, u32[]{:S(2)}) %collective-permute-start.1) | collective-permute-done | bytes 262176 | tf_op jit(solution)/shard_map/ppermute | solution.py:408
  12.4 3.1 %collective-permute-start.4 = (f32[4,16,512]{2,1,0:T(8,128)S(1)}, f32[4,16,512]{2,1,0:T(8,128)S(1)}, u32[]{:S(2)}, u32[]{:S(2)}) collective-permute-start(f32[4,16,512]{2,1,0:T(8,128)S(1)} %collective-permute-done.one_ref.refs_1_), channel_id=1, source_target_pairs={{0,2},{1,3},{4,6},{5,7},{8,10},{9,11},{12,14},{13,15},{18,16},{19,... | collective-permute-start | bytes 393224 | tf_op jit(solution)/shard_map/ppermute | solution.py:408
  15.8 1.1 %collective-permute-start.8 = (f32[4,16,512]{2,1,0:T(8,128)S(1)}, f32[4,16,512]{2,1,0:T(8,128)S(1)}, u32[]{:S(2)}, u32[]{:S(2)}) collective-permute-start(f32[4,16,512]{2,1,0:T(8,128)S(1)} %slice.6), channel_id=1, source_target_pairs={{0,4},{1,5},{2,6},{3,7},{4,0},{5,1},{6,2},{7,3},{8,12},{9,13},{10,... | collective-permute-start | bytes 393224 | tf_op jit(solution)/shard_map/ppermute | solution.py:408
  16.9 1.3 %collective-permute-start.9 = (f32[4,16,512]{2,1,0:T(8,128)S(1)}, f32[4,16,512]{2,1,0:T(8,128)S(1)}, u32[]{:S(2)}, u32[]{:S(2)}) collective-permute-start(f32[4,16,512]{2,1,0:T(8,128)S(1)} %slice.7), channel_id=1, source_target_pairs={{0,8},{1,9},{2,10},{3,11},{4,12},{5,13},{6,14},{7,15},{8,0},{9,1},... | collective-permute-start | bytes 393224 | tf_op jit(solution)/shard_map/ppermute | solution.py:408
  18.3 1.2 %shard_map.65 = (f32[4,16,1536]{2,1,0:T(8,128)S(1)}, f32[16,16,1024]{2,1,0:T(8,128)S(1)}) custom-call(bf16[512,1024]{1,0:T(8,128)(2,1)S(1)} %get-tuple-element.44.high_ref, bf16[512,1024]{1,0:T(8,128)(2,1)S(1)} %get-tuple-element.45.low_ref, f32[4,16,512]{2,1,0:T(8,128)S(1)} %collective-permute-done.one_ref.refs_1_, ...), custom_call_target="tpu_custom_call" | custom-call | tf_op jit(solution)/shard_map/pallas_call | solution.py:384
  19.4 2.2 %collective-permute-done.6.weights_ref = f32[88,128]{1,0:T(8,128)S(1)} collective-permute-done((f32[88,128]{1,0:T(8,128)S(1)}, f32[88,128]{1,0:T(8,128)S(1)}, u32[]{:S(2)}, u32[]{:S(2)}) %collective-permute-start.6) | collective-permute-done | bytes 45088 | tf_op jit(solution)/shard_map/ppermute | solution.py:408
  21.6 0.7 %collective-permute-start.7 = (f32[4,16,512]{2,1,0:T(8,128)S(1)}, f32[4,16,512]{2,1,0:T(8,128)S(1)}, u32[]{:S(2)}, u32[]{:S(2)}) collective-permute-start(f32[4,16,512]{2,1,0:T(8,128)S(1)} %collective-permute-done.4.refs_0_.refs_2_), channel_id=1, source_target_pairs={{2,3},{3,2},{6,7},{7,6},{10,11},{11,10},{14,15},{15,14},{16,17},{1... | collective-permute-start | bytes 393224 | tf_op jit(solution)/shard_map/ppermute | solution.py:408
  22.3 1.1 %collective-permute-done.9.refs_4_ = f32[4,16,512]{2,1,0:T(8,128)S(1)} collective-permute-done((f32[4,16,512]{2,1,0:T(8,128)S(1)}, f32[4,16,512]{2,1,0:T(8,128)S(1)}, u32[]{:S(2)}, u32[]{:S(2)}) %collective-permute-start.9) | collective-permute-done | bytes 131104 | tf_op jit(solution)/shard_map/ppermute | solution.py:408
  23.4 1.1 %collective-permute-start.10 = (f32[2,32,512]{2,1,0:T(8,128)S(1)}, f32[2,32,512]{2,1,0:T(8,128)S(1)}, u32[]{:S(2)}, u32[]{:S(2)}) collective-permute-start(f32[2,32,512]{2,1,0:T(8,128)S(1)} %get-tuple-element.66), channel_id=1, source_target_pairs={{0,4},{1,5},{2,6},{3,7},{4,0},{5,1},{6,2},{7,3},{8,12},{9,13},{10,... | collective-permute-start | bytes 393224 | tf_op jit(solution)/shard_map/ppermute | solution.py:408
  24.5 0.9 %collective-permute-start.11 = (f32[2,32,512]{2,1,0:T(8,128)S(1)}, f32[2,32,512]{2,1,0:T(8,128)S(1)}, u32[]{:S(2)}, u32[]{:S(2)}) collective-permute-start(f32[2,32,512]{2,1,0:T(8,128)S(1)} %get-tuple-element.67), channel_id=1, source_target_pairs={{0,12},{1,13},{2,14},{3,15},{4,8},{5,9},{6,10},{7,11},{8,4},{9,5},... | collective-permute-start | bytes 393224 | tf_op jit(solution)/shard_map/ppermute | solution.py:408
  25.4 4.1 %shard_map.66 = (f32[2,16,512]{2,1,0:T(8,128)S(1)}, f32[2,16,512]{2,1,0:T(8,128)S(1)}, f32[32,16,1536]{2,1,0:T(8,128)S(1)}) custom-call(s32[21]{0:T(128)S(1)} %copy-done.6, bf16[512,1024]{1,0:T(8,128)(2,1)S(1)} %get-tuple-element.44.high_ref, bf16[512,1024]{1,0:T(8,128)(2,1)S(1)} %get-tuple-element.45.low_ref, ...), custom_call_target="tpu_custom_call" | custom-call | tf_op jit(solution)/shard_map/pallas_call | solution.py:384
  29.5 2.7 %collective-permute-start.12 = (f32[2,16,512]{2,1,0:T(8,128)S(1)}, f32[2,16,512]{2,1,0:T(8,128)S(1)}, u32[]{:S(2)}, u32[]{:S(2)}) collective-permute-start(f32[2,16,512]{2,1,0:T(8,128)S(1)} %get-tuple-element.70), channel_id=1, source_target_pairs={{0,16},{1,17},{2,18},{3,19},{4,20},{5,21},{6,22},{7,23},{8,24},{9,... | collective-permute-start | bytes 196616 | tf_op jit(solution)/shard_map/ppermute | solution.py:408
  32.2 2.3 %shard_map.68 = (f32[2,16,512]{2,1,0:T(8,128)S(1)}, f32[4,32,1536]{2,1,0:T(8,128)S(1)}) custom-call(s32[21]{0:T(128)S(1)} %copy-done.6, bf16[512,1024]{1,0:T(8,128)(2,1)S(1)} %get-tuple-element.44.high_ref, bf16[512,1024]{1,0:T(8,128)(2,1)S(1)} %get-tuple-element.45.low_ref, f32[88,128]{1,0:T(8,128)S(1)} %collective-permute-done.6.weights_ref, ...), custom_call_target="tpu_custom_call" | custom-call | tf_op jit(solution)/shard_map/pallas_call | solution.py:384
  34.5 2.0 %collective-permute-start.13 = (f32[2,16,512]{2,1,0:T(8,128)S(1)}, f32[2,16,512]{2,1,0:T(8,128)S(1)}, u32[]{:S(2)}, u32[]{:S(2)}) collective-permute-start(f32[2,16,512]{2,1,0:T(8,128)S(1)} %get-tuple-element.72), channel_id=1, source_target_pairs={{0,16},{1,17},{2,18},{3,19},{4,20},{5,21},{6,22},{7,23},{8,24},{9,... | collective-permute-start | bytes 196616 | tf_op jit(solution)/shard_map/ppermute | solution.py:408
  36.5 4.4 %shard_map.69.part_ref = f32[4,16,512]{2,1,0:T(8,128)S(1)} custom-call(s32[21]{0:T(128)S(1)} %copy-done.6, bf16[512,1024]{1,0:T(8,128)(2,1)S(1)} %get-tuple-element.44.high_ref, bf16[512,1024]{1,0:T(8,128)(2,1)S(1)} %get-tuple-element.45.low_ref, f32[88,128]{1,0:T(8,128)S(1)} %get-tuple-element.46.weights_ref, ...), custom_call_target="tpu_custom_call" | custom-call | tf_op jit(solution)/shard_map/pallas_call | solution.py:384
  40.9 0.7 %shard_map.70 = f32[4,16,512]{2,1,0:T(8,128)} custom-call(f32[4,16,512]{2,1,0:T(8,128)S(1)} %shard_map.69.part_ref, f32[2,16,512]{2,1,0:T(8,128)S(1)} %collective-permute-done.13.ends_ref), custom_call_target="tpu_custom_call" | custom-call | tf_op jit(solution)/shard_map/pallas_call | solution.py:384
  (27 shorter events, 0.4 us)
Async XLA Ops:
  0.0 25.4 %copy-start.6 = (s32[21]{0:T(128)S(1)}, s32[21]{0:T(128)}, u32[]{:S(2)}) copy-start(s32[21]{0:T(128)} %offsets_from.5) | copy-start | bytes 256
  0.0 12.3 %collective-permute-start.1 = (f32[8,16,512]{2,1,0:T(8,128)}, f32[8,16,512]{2,1,0:T(8,128)S(1)}, u32[]{:S(2)}, u32[]{:S(2)}) collective-permute-start(f32[8,16,512]{2,1,0:T(8,128)} %right_ref.1), channel_id=1, source_target_pairs={{0,8},{1,9},{2,10},{3,11},{4,12},{5,13},{6,14},{7,15},{8,0},{9,1},... | collective-permute-start | bytes 786440 | tf_op jit(solution)/shard_map/ppermute | solution.py:408
  3.0 9.3 %collective-permute-start.2 = (f32[8,16,512]{2,1,0:T(8,128)}, f32[8,16,512]{2,1,0:T(8,128)S(1)}, u32[]{:S(2)}, u32[]{:S(2)}) collective-permute-start(f32[8,16,512]{2,1,0:T(8,128)} %right_ref.1), channel_id=1, source_target_pairs={{0,4},{1,5},{2,6},{3,7},{4,0},{5,1},{6,2},{7,3},{8,12},{9,13},{10,... | collective-permute-start | bytes 786440 | tf_op jit(solution)/shard_map/ppermute | solution.py:408
  4.5 6.4 %collective-permute-start = (f32[4,16,512]{2,1,0:T(8,128)}, f32[4,16,512]{2,1,0:T(8,128)S(1)}, u32[]{:S(2)}, u32[]{:S(2)}) collective-permute-start(f32[4,16,512]{2,1,0:T(8,128)} %refs_0_.1), channel_id=1, source_target_pairs={{0,2},{1,3},{2,18},{3,19},{4,6},{5,7},{6,22},{7,23},{8,10},{9,11},... | collective-permute-start | bytes 393224 | tf_op jit(solution)/shard_map/ppermute | solution.py:408
  6.0 4.9 %collective-permute-start.3 = (f32[4,16,512]{2,1,0:T(8,128)}, f32[4,16,512]{2,1,0:T(8,128)S(1)}, u32[]{:S(2)}, u32[]{:S(2)}) collective-permute-start(f32[4,16,512]{2,1,0:T(8,128)} %refs_0_.1), channel_id=1, source_target_pairs={{0,1},{1,0},{2,3},{3,2},{4,5},{5,4},{6,7},{7,6},{8,9},{9,8},{10,11... | collective-permute-start | bytes 393224 | tf_op jit(solution)/shard_map/ppermute | solution.py:408
  6.0 0.9 %copy-start = (f32[4,16,512]{2,1,0:T(8,128)S(1)}, f32[4,16,512]{2,1,0:T(8,128)}, u32[]{:S(2)}) copy-start(f32[4,16,512]{2,1,0:T(8,128)} %refs_0_.1) | copy-start | bytes 393220
  7.0 0.9 %copy-start.2 = (f32[8,16,512]{2,1,0:T(8,128)S(1)}, f32[8,16,512]{2,1,0:T(8,128)}, u32[]{:S(2)}) copy-start(f32[8,16,512]{2,1,0:T(8,128)} %right_ref.1) | copy-start | bytes 786436
  7.9 0.9 %copy-start.3 = (f32[96,512]{1,0:T(8,128)S(1)}, f32[96,512]{1,0:T(8,128)}, u32[]{:S(2)}) copy-start(f32[96,512]{1,0:T(8,128)} %constant.2.clone.phases_ref) | copy-start | bytes 589828
  8.9 0.9 %copy-start.5 = (f32[3,21,4,16]{1,3,2,0:T(8,128)S(1)}, f32[3,21,4,16]{1,3,2,0:T(8,128)}, u32[]{:S(2)}) copy-start(f32[3,21,4,16]{1,3,2,0:T(8,128)} %param.9) | copy-start | bytes 48388
  9.7 13.6 %copy-start.1 = (f32[4,16,512]{2,1,0:T(8,128)S(1)}, f32[4,16,512]{2,1,0:T(8,128)}, u32[]{:S(2)}) copy-start(f32[4,16,512]{2,1,0:T(8,128)} %refs_0_.1) | copy-start | bytes 393220
  12.4 9.2 %collective-permute-start.4 = (f32[4,16,512]{2,1,0:T(8,128)S(1)}, f32[4,16,512]{2,1,0:T(8,128)S(1)}, u32[]{:S(2)}, u32[]{:S(2)}) collective-permute-start(f32[4,16,512]{2,1,0:T(8,128)S(1)} %collective-permute-done.one_ref.refs_1_), channel_id=1, source_target_pairs={{0,2},{1,3},{4,6},{5,7},{8,10},{9,11},{12,14},{13,15},{18,16},{19,... | collective-permute-start | bytes 393224 | tf_op jit(solution)/shard_map/ppermute | solution.py:408
  15.5 6.1 %collective-permute-start.5 = (f32[4,16,512]{2,1,0:T(8,128)S(1)}, f32[4,16,512]{2,1,0:T(8,128)S(1)}, u32[]{:S(2)}, u32[]{:S(2)}) collective-permute-start(f32[4,16,512]{2,1,0:T(8,128)S(1)} %collective-permute-done.one_ref.refs_1_), channel_id=1, source_target_pairs={{0,1},{1,0},{2,3},{3,2},{4,5},{5,4},{6,7},{7,6},{8,9},{9,8},{10,11... | collective-permute-start | bytes 393224 | tf_op jit(solution)/shard_map/ppermute | solution.py:408
  15.8 5.8 %collective-permute-start.6 = (f32[88,128]{1,0:T(8,128)S(1)}, f32[88,128]{1,0:T(8,128)S(1)}, u32[]{:S(2)}, u32[]{:S(2)}) collective-permute-start(f32[88,128]{1,0:T(8,128)S(1)} %get-tuple-element.46.weights_ref), channel_id=1, source_target_pairs={{0,16},{1,17},{2,18},{3,19},{4,20},{5,21},{6,22},{7,23},{8,24},{9,... | collective-permute-start | bytes 135176 | tf_op jit(solution)/shard_map/ppermute | solution.py:408
  15.8 6.5 %collective-permute-start.8 = (f32[4,16,512]{2,1,0:T(8,128)S(1)}, f32[4,16,512]{2,1,0:T(8,128)S(1)}, u32[]{:S(2)}, u32[]{:S(2)}) collective-permute-start(f32[4,16,512]{2,1,0:T(8,128)S(1)} %slice.6), channel_id=1, source_target_pairs={{0,4},{1,5},{2,6},{3,7},{4,0},{5,1},{6,2},{7,3},{8,12},{9,13},{10,... | collective-permute-start | bytes 393224 | tf_op jit(solution)/shard_map/ppermute | solution.py:408
  16.9 6.4 %collective-permute-start.9 = (f32[4,16,512]{2,1,0:T(8,128)S(1)}, f32[4,16,512]{2,1,0:T(8,128)S(1)}, u32[]{:S(2)}, u32[]{:S(2)}) collective-permute-start(f32[4,16,512]{2,1,0:T(8,128)S(1)} %slice.7), channel_id=1, source_target_pairs={{0,8},{1,9},{2,10},{3,11},{4,12},{5,13},{6,14},{7,15},{8,0},{9,1},... | collective-permute-start | bytes 393224 | tf_op jit(solution)/shard_map/ppermute | solution.py:408
  21.6 1.7 %collective-permute-start.7 = (f32[4,16,512]{2,1,0:T(8,128)S(1)}, f32[4,16,512]{2,1,0:T(8,128)S(1)}, u32[]{:S(2)}, u32[]{:S(2)}) collective-permute-start(f32[4,16,512]{2,1,0:T(8,128)S(1)} %collective-permute-done.4.refs_0_.refs_2_), channel_id=1, source_target_pairs={{2,3},{3,2},{6,7},{7,6},{10,11},{11,10},{14,15},{15,14},{16,17},{1... | collective-permute-start | bytes 393224 | tf_op jit(solution)/shard_map/ppermute | solution.py:408
  23.4 8.8 %collective-permute-start.10 = (f32[2,32,512]{2,1,0:T(8,128)S(1)}, f32[2,32,512]{2,1,0:T(8,128)S(1)}, u32[]{:S(2)}, u32[]{:S(2)}) collective-permute-start(f32[2,32,512]{2,1,0:T(8,128)S(1)} %get-tuple-element.66), channel_id=1, source_target_pairs={{0,4},{1,5},{2,6},{3,7},{4,0},{5,1},{6,2},{7,3},{8,12},{9,13},{10,... | collective-permute-start | bytes 393224 | tf_op jit(solution)/shard_map/ppermute | solution.py:408
  24.5 7.7 %collective-permute-start.11 = (f32[2,32,512]{2,1,0:T(8,128)S(1)}, f32[2,32,512]{2,1,0:T(8,128)S(1)}, u32[]{:S(2)}, u32[]{:S(2)}) collective-permute-start(f32[2,32,512]{2,1,0:T(8,128)S(1)} %get-tuple-element.67), channel_id=1, source_target_pairs={{0,12},{1,13},{2,14},{3,15},{4,8},{5,9},{6,10},{7,11},{8,4},{9,5},... | collective-permute-start | bytes 393224 | tf_op jit(solution)/shard_map/ppermute | solution.py:408
  29.5 7.0 %copy-start.4 = (f32[4,16,512]{2,1,0:T(8,128)S(1)}, f32[4,16,512]{2,1,0:T(8,128)}, u32[]{:S(2)}) copy-start(f32[4,16,512]{2,1,0:T(8,128)} %recorded_ref.1) | copy-start | bytes 393220
  29.5 7.0 %collective-permute-start.12 = (f32[2,16,512]{2,1,0:T(8,128)S(1)}, f32[2,16,512]{2,1,0:T(8,128)S(1)}, u32[]{:S(2)}, u32[]{:S(2)}) collective-permute-start(f32[2,16,512]{2,1,0:T(8,128)S(1)} %get-tuple-element.70), channel_id=1, source_target_pairs={{0,16},{1,17},{2,18},{3,19},{4,20},{5,21},{6,22},{7,23},{8,24},{9,... | collective-permute-start | bytes 196616 | tf_op jit(solution)/shard_map/ppermute | solution.py:408
  34.5 6.4 %collective-permute-start.13 = (f32[2,16,512]{2,1,0:T(8,128)S(1)}, f32[2,16,512]{2,1,0:T(8,128)S(1)}, u32[]{:S(2)}, u32[]{:S(2)}) collective-permute-start(f32[2,16,512]{2,1,0:T(8,128)S(1)} %get-tuple-element.72), channel_id=1, source_target_pairs={{0,16},{1,17},{2,18},{3,19},{4,20},{5,21},{6,22},{7,23},{8,24},{9,... | collective-permute-start | bytes 196616 | tf_op jit(solution)/shard_map/ppermute | solution.py:408

commit v4 on v3

--- a/solution.py
+++ b/solution.py
@@ -439,7 +439,7 @@
     ones = [permute(one, lambda i, j, k=k: (i, j ^ k)) for k in range(1, slots)]
     rest = []
     for k in range(cut, blocks):
-        bits = [1 << n for n in range(blocks) if 0 < k ^ (1 << n) < cut][:2]
+        bits = [1 << n for n in range(blocks) if 0 < k ^ (1 << n) < cut][1::-1]
         part = right_count // len(bits)
         for n, bit in enumerate(bits):
             of = some[(k ^ bit) - 1][n * part : (n + 1) * part if n + 1 < len(bits) else None]
@@ -449,8 +449,8 @@
         second_kernel, [high, low, one] + some,
         [left_shape, (len(some) * right_count, sources, width)], [],
     )
-    two, ones, mirror_weights, one_spectra, right_b = lax.optimization_barrier(
-        (two, ones, mirror_weights, one_spectra, right_b)
+    ones, two, mirror_weights, one_spectra, right_b = lax.optimization_barrier(
+        (ones, two, mirror_weights, one_spectra, right_b)
     )
     gathered = [two]
     for k in range(1, slots):

time: 41.8 us -> 41.8 us (level)
  waiting for transfers between devices: 4.62 us -> 3.64 us
  starting transfers between devices: 19.3 us -> 20.2 us
    ppermute x14, waiting for transfers between devices: 4.62 us -> 3.64 us  [permute(): return lax.ppermute(array, AXES, pairs)]
    ppermute x14, starting transfers between devices: 19.3 us -> 20.2 us  [permute(): return lax.ppermute(array, AXES, pairs)]
where the time goes in v4:
time: 41.8 us; the launch traced here: 41.5 us
  starting transfers between devices  20.2 us (48%)
  Pallas kernels  13.8 us (33%)
  local copies, waits for them, and re-layouts  3.74 us (9%)
  waiting for transfers between devices  3.64 us (9%)
    ppermute x14, starting transfers between devices, permute(): return lax.ppermute(array, AXES, pairs)  20.2 us
    pallas_call x7, Pallas kernels, call(): pl.pallas_call(kernel, out_shape=shapes, in_specs=[pl.BlockSpec(memory_sp...  13.8 us
    unnamed x14, local copies, waits for them, and re-layouts  3.72 us
    ppermute x14, waiting for transfers between devices, permute(): return lax.ppermute(array, AXES, pairs)  3.64 us
  transfers between devices with their start and end apart: 14, of which 3 were waited for; matrix products, arithmetic and copies ran while one was open for 0% of the time, Pallas kernels for 32%

profile of v4, /device:TPU:0, one launch (start us, length us, event | category | flops | bytes accessed | tf_op | source)
XLA Modules:
  0.0 41.5 jit_solution(14483080801028068569)
XLA Ops:
  0.0 3.0 %collective-permute-start.1 = (f32[8,16,512]{2,1,0:T(8,128)}, f32[8,16,512]{2,1,0:T(8,128)S(1)}, u32[]{:S(2)}, u32[]{:S(2)}) collective-permute-start(f32[8,16,512]{2,1,0:T(8,128)} %right_ref.1), channel_id=1, source_target_pairs={{0,8},{1,9},{2,10},{3,11},{4,12},{5,13},{6,14},{7,15},{8,0},{9,1},... | collective-permute-start | bytes 786440 | tf_op jit(solution)/shard_map/ppermute | solution.py:408
  3.0 1.5 %collective-permute-start.2 = (f32[8,16,512]{2,1,0:T(8,128)}, f32[8,16,512]{2,1,0:T(8,128)S(1)}, u32[]{:S(2)}, u32[]{:S(2)}) collective-permute-start(f32[8,16,512]{2,1,0:T(8,128)} %right_ref.1), channel_id=1, source_target_pairs={{0,4},{1,5},{2,6},{3,7},{4,0},{5,1},{6,2},{7,3},{8,12},{9,13},{10,... | collective-permute-start | bytes 786440 | tf_op jit(solution)/shard_map/ppermute | solution.py:408
  4.5 1.5 %collective-permute-start = (f32[4,16,512]{2,1,0:T(8,128)}, f32[4,16,512]{2,1,0:T(8,128)S(1)}, u32[]{:S(2)}, u32[]{:S(2)}) collective-permute-start(f32[4,16,512]{2,1,0:T(8,128)} %refs_0_.1), channel_id=1, source_target_pairs={{0,2},{1,3},{2,18},{3,19},{4,6},{5,7},{6,22},{7,23},{8,10},{9,11},... | collective-permute-start | bytes 393224 | tf_op jit(solution)/shard_map/ppermute | solution.py:408
  6.0 0.9 %copy-done = f32[4,16,512]{2,1,0:T(8,128)S(1)} copy-done((f32[4,16,512]{2,1,0:T(8,128)S(1)}, f32[4,16,512]{2,1,0:T(8,128)}, u32[]{:S(2)}) %copy-start) | copy-done | bytes 131096
  7.0 0.9 %copy-done.2 = f32[8,16,512]{2,1,0:T(8,128)S(1)} copy-done((f32[8,16,512]{2,1,0:T(8,128)S(1)}, f32[8,16,512]{2,1,0:T(8,128)}, u32[]{:S(2)}) %copy-start.2) | copy-done | bytes 262168
  7.9 0.9 %copy-done.3 = f32[96,512]{1,0:T(8,128)S(1)} copy-done((f32[96,512]{1,0:T(8,128)S(1)}, f32[96,512]{1,0:T(8,128)}, u32[]{:S(2)}) %copy-start.3) | copy-done | bytes 196632
  8.9 0.9 %copy-done.5 = f32[3,21,4,16]{1,3,2,0:T(8,128)S(1)} copy-done((f32[3,21,4,16]{1,3,2,0:T(8,128)S(1)}, f32[3,21,4,16]{1,3,2,0:T(8,128)}, u32[]{:S(2)}) %copy-start.5) | copy-done | bytes 16152
  9.8 1.2 %shard_map.64 = (bf16[512,1024]{1,0:T(8,128)(2,1)S(1)}, bf16[512,1024]{1,0:T(8,128)(2,1)S(1)}, f32[88,128]{1,0:T(8,128)S(1)}, f32[4,16,1536]{2,1,0:T(8,128)S(1)}, f32[8,16,1024]{2,1,0:T(8,128)S(1)}) custom-call(f32[96,512]{1,0:T(8,128)S(1)} %copy-done.3, f32[3,4,16,21]{3,2,1,0:T(8,128)S(1)} %bitcast.1, f32[4,16,512]{2,1,0:T(8,128)S(1)} %copy-done, ...), custom_call_target="tpu_custom_call" | custom-call | tf_op jit(solution)/shard_map/pallas_call | solution.py:384
  11.0 1.4 %collective-permute-done.1.refs_1_ = f32[8,16,512]{2,1,0:T(8,128)S(1)} collective-permute-done((f32[8,16,512]{2,1,0:T(8,128)}, f32[8,16,512]{2,1,0:T(8,128)S(1)}, u32[]{:S(2)}, u32[]{:S(2)}) %collective-permute-start.1) | collective-permute-done | bytes 262176 | tf_op jit(solution)/shard_map/ppermute | solution.py:408
  12.4 3.7 %collective-permute-start.5 = (f32[4,16,512]{2,1,0:T(8,128)S(1)}, f32[4,16,512]{2,1,0:T(8,128)S(1)}, u32[]{:S(2)}, u32[]{:S(2)}) collective-permute-start(f32[4,16,512]{2,1,0:T(8,128)S(1)} %collective-permute-done.one_ref.refs_1_), channel_id=1, source_target_pairs={{0,2},{1,3},{4,6},{5,7},{8,10},{9,11},{12,14},{13,15},{18,16},{19,... | collective-permute-start | bytes 393224 | tf_op jit(solution)/shard_map/ppermute | solution.py:408
  16.1 0.5 %collective-permute-start.8 = (f32[4,16,512]{2,1,0:T(8,128)S(1)}, f32[4,16,512]{2,1,0:T(8,128)S(1)}, u32[]{:S(2)}, u32[]{:S(2)}) collective-permute-start(f32[4,16,512]{2,1,0:T(8,128)S(1)} %slice.6), channel_id=1, source_target_pairs={{0,8},{1,9},{2,10},{3,11},{4,12},{5,13},{6,14},{7,15},{8,0},{9,1},... | collective-permute-start | bytes 393224 | tf_op jit(solution)/shard_map/ppermute | solution.py:408
  16.7 1.6 %collective-permute-start.9 = (f32[4,16,512]{2,1,0:T(8,128)S(1)}, f32[4,16,512]{2,1,0:T(8,128)S(1)}, u32[]{:S(2)}, u32[]{:S(2)}) collective-permute-start(f32[4,16,512]{2,1,0:T(8,128)S(1)} %slice.7), channel_id=1, source_target_pairs={{0,4},{1,5},{2,6},{3,7},{4,0},{5,1},{6,2},{7,3},{8,12},{9,13},{10,... | collective-permute-start | bytes 393224 | tf_op jit(solution)/shard_map/ppermute | solution.py:408
  18.3 1.2 %shard_map.65 = (f32[4,16,1536]{2,1,0:T(8,128)S(1)}, f32[16,16,1024]{2,1,0:T(8,128)S(1)}) custom-call(bf16[512,1024]{1,0:T(8,128)(2,1)S(1)} %get-tuple-element.44.high_ref, bf16[512,1024]{1,0:T(8,128)(2,1)S(1)} %get-tuple-element.45.low_ref, f32[4,16,512]{2,1,0:T(8,128)S(1)} %collective-permute-done.one_ref.refs_1_, ...), custom_call_target="tpu_custom_call" | custom-call | tf_op jit(solution)/shard_map/pallas_call | solution.py:384
  19.4 2.1 %collective-permute-done.6.weights_ref = f32[88,128]{1,0:T(8,128)S(1)} collective-permute-done((f32[88,128]{1,0:T(8,128)S(1)}, f32[88,128]{1,0:T(8,128)S(1)}, u32[]{:S(2)}, u32[]{:S(2)}) %collective-permute-start.6) | collective-permute-done | bytes 45088 | tf_op jit(solution)/shard_map/ppermute | solution.py:408
  21.5 0.7 %collective-permute-start.7 = (f32[4,16,512]{2,1,0:T(8,128)S(1)}, f32[4,16,512]{2,1,0:T(8,128)S(1)}, u32[]{:S(2)}, u32[]{:S(2)}) collective-permute-start(f32[4,16,512]{2,1,0:T(8,128)S(1)} %collective-permute-done.5.refs_0_.refs_2_), channel_id=1, source_target_pairs={{2,3},{3,2},{6,7},{7,6},{10,11},{11,10},{14,15},{15,14},{16,17},{1... | collective-permute-start | bytes 393224 | tf_op jit(solution)/shard_map/ppermute | solution.py:408
  22.2 0.1 collective-permute-done.8.refs_3_
  22.4 1.6 %collective-permute-start.10 = (f32[2,32,512]{2,1,0:T(8,128)S(1)}, f32[2,32,512]{2,1,0:T(8,128)S(1)}, u32[]{:S(2)}, u32[]{:S(2)}) collective-permute-start(f32[2,32,512]{2,1,0:T(8,128)S(1)} %get-tuple-element.66), channel_id=1, source_target_pairs={{0,4},{1,5},{2,6},{3,7},{4,0},{5,1},{6,2},{7,3},{8,12},{9,13},{10,... | collective-permute-start | bytes 393224 | tf_op jit(solution)/shard_map/ppermute | solution.py:408
  24.0 0.9 %collective-permute-start.11 = (f32[2,32,512]{2,1,0:T(8,128)S(1)}, f32[2,32,512]{2,1,0:T(8,128)S(1)}, u32[]{:S(2)}, u32[]{:S(2)}) collective-permute-start(f32[2,32,512]{2,1,0:T(8,128)S(1)} %get-tuple-element.67), channel_id=1, source_target_pairs={{0,12},{1,13},{2,14},{3,15},{4,8},{5,9},{6,10},{7,11},{8,4},{9,5},... | collective-permute-start | bytes 393224 | tf_op jit(solution)/shard_map/ppermute | solution.py:408
  24.8 4.0 %shard_map.66 = (f32[2,16,512]{2,1,0:T(8,128)S(1)}, f32[2,16,512]{2,1,0:T(8,128)S(1)}, f32[32,16,1536]{2,1,0:T(8,128)S(1)}) custom-call(s32[21]{0:T(128)S(1)} %copy-done.6, bf16[512,1024]{1,0:T(8,128)(2,1)S(1)} %get-tuple-element.44.high_ref, bf16[512,1024]{1,0:T(8,128)(2,1)S(1)} %get-tuple-element.45.low_ref, ...), custom_call_target="tpu_custom_call" | custom-call | tf_op jit(solution)/shard_map/pallas_call | solution.py:384
  28.9 3.6 %collective-permute-start.12 = (f32[2,16,512]{2,1,0:T(8,128)S(1)}, f32[2,16,512]{2,1,0:T(8,128)S(1)}, u32[]{:S(2)}, u32[]{:S(2)}) collective-permute-start(f32[2,16,512]{2,1,0:T(8,128)S(1)} %get-tuple-element.70), channel_id=1, source_target_pairs={{0,16},{1,17},{2,18},{3,19},{4,20},{5,21},{6,22},{7,23},{8,24},{9,... | collective-permute-start | bytes 196616 | tf_op jit(solution)/shard_map/ppermute | solution.py:408
  32.6 2.3 %shard_map.68 = (f32[2,16,512]{2,1,0:T(8,128)S(1)}, f32[4,32,1536]{2,1,0:T(8,128)S(1)}) custom-call(s32[21]{0:T(128)S(1)} %copy-done.6, bf16[512,1024]{1,0:T(8,128)(2,1)S(1)} %get-tuple-element.44.high_ref, bf16[512,1024]{1,0:T(8,128)(2,1)S(1)} %get-tuple-element.45.low_ref, f32[88,128]{1,0:T(8,128)S(1)} %collective-permute-done.6.weights_ref, ...), custom_call_target="tpu_custom_call" | custom-call | tf_op jit(solution)/shard_map/pallas_call | solution.py:384
  34.9 1.6 %collective-permute-start.13 = (f32[2,16,512]{2,1,0:T(8,128)S(1)}, f32[2,16,512]{2,1,0:T(8,128)S(1)}, u32[]{:S(2)}, u32[]{:S(2)}) collective-permute-start(f32[2,16,512]{2,1,0:T(8,128)S(1)} %get-tuple-element.72), channel_id=1, source_target_pairs={{0,16},{1,17},{2,18},{3,19},{4,20},{5,21},{6,22},{7,23},{8,24},{9,... | collective-permute-start | bytes 196616 | tf_op jit(solution)/shard_map/ppermute | solution.py:408
  36.5 4.4 %shard_map.69.part_ref = f32[4,16,512]{2,1,0:T(8,128)S(1)} custom-call(s32[21]{0:T(128)S(1)} %copy-done.6, bf16[512,1024]{1,0:T(8,128)(2,1)S(1)} %get-tuple-element.44.high_ref, bf16[512,1024]{1,0:T(8,128)(2,1)S(1)} %get-tuple-element.45.low_ref, f32[88,128]{1,0:T(8,128)S(1)} %get-tuple-element.46.weights_ref, ...), custom_call_target="tpu_custom_call" | custom-call | tf_op jit(solution)/shard_map/pallas_call | solution.py:384
  40.9 0.7 %shard_map.70 = f32[4,16,512]{2,1,0:T(8,128)} custom-call(f32[4,16,512]{2,1,0:T(8,128)S(1)} %shard_map.69.part_ref, f32[2,16,512]{2,1,0:T(8,128)S(1)} %collective-permute-done.13.ends_ref), custom_call_target="tpu_custom_call" | custom-call | tf_op jit(solution)/shard_map/pallas_call | solution.py:384
  (27 shorter events, 0.2 us)
Async XLA Ops:
  0.0 24.8 %copy-start.6 = (s32[21]{0:T(128)S(1)}, s32[21]{0:T(128)}, u32[]{:S(2)}) copy-start(s32[21]{0:T(128)} %offsets_from.5) | copy-start | bytes 256
  0.0 12.3 %collective-permute-start.1 = (f32[8,16,512]{2,1,0:T(8,128)}, f32[8,16,512]{2,1,0:T(8,128)S(1)}, u32[]{:S(2)}, u32[]{:S(2)}) collective-permute-start(f32[8,16,512]{2,1,0:T(8,128)} %right_ref.1), channel_id=1, source_target_pairs={{0,8},{1,9},{2,10},{3,11},{4,12},{5,13},{6,14},{7,15},{8,0},{9,1},... | collective-permute-start | bytes 786440 | tf_op jit(solution)/shard_map/ppermute | solution.py:408
  3.0 9.3 %collective-permute-start.2 = (f32[8,16,512]{2,1,0:T(8,128)}, f32[8,16,512]{2,1,0:T(8,128)S(1)}, u32[]{:S(2)}, u32[]{:S(2)}) collective-permute-start(f32[8,16,512]{2,1,0:T(8,128)} %right_ref.1), channel_id=1, source_target_pairs={{0,4},{1,5},{2,6},{3,7},{4,0},{5,1},{6,2},{7,3},{8,12},{9,13},{10,... | collective-permute-start | bytes 786440 | tf_op jit(solution)/shard_map/ppermute | solution.py:408
  4.5 6.4 %collective-permute-start = (f32[4,16,512]{2,1,0:T(8,128)}, f32[4,16,512]{2,1,0:T(8,128)S(1)}, u32[]{:S(2)}, u32[]{:S(2)}) collective-permute-start(f32[4,16,512]{2,1,0:T(8,128)} %refs_0_.1), channel_id=1, source_target_pairs={{0,2},{1,3},{2,18},{3,19},{4,6},{5,7},{6,22},{7,23},{8,10},{9,11},... | collective-permute-start | bytes 393224 | tf_op jit(solution)/shard_map/ppermute | solution.py:408
  6.0 4.9 %collective-permute-start.3 = (f32[4,16,512]{2,1,0:T(8,128)}, f32[4,16,512]{2,1,0:T(8,128)S(1)}, u32[]{:S(2)}, u32[]{:S(2)}) collective-permute-start(f32[4,16,512]{2,1,0:T(8,128)} %refs_0_.1), channel_id=1, source_target_pairs={{0,1},{1,0},{2,3},{3,2},{4,5},{5,4},{6,7},{7,6},{8,9},{9,8},{10,11... | collective-permute-start | bytes 393224 | tf_op jit(solution)/shard_map/ppermute | solution.py:408
  6.0 0.9 %copy-start = (f32[4,16,512]{2,1,0:T(8,128)S(1)}, f32[4,16,512]{2,1,0:T(8,128)}, u32[]{:S(2)}) copy-start(f32[4,16,512]{2,1,0:T(8,128)} %refs_0_.1) | copy-start | bytes 393220
  7.0 0.9 %copy-start.2 = (f32[8,16,512]{2,1,0:T(8,128)S(1)}, f32[8,16,512]{2,1,0:T(8,128)}, u32[]{:S(2)}) copy-start(f32[8,16,512]{2,1,0:T(8,128)} %right_ref.1) | copy-start | bytes 786436
  7.9 0.9 %copy-start.3 = (f32[96,512]{1,0:T(8,128)S(1)}, f32[96,512]{1,0:T(8,128)}, u32[]{:S(2)}) copy-start(f32[96,512]{1,0:T(8,128)} %constant.2.clone.phases_ref) | copy-start | bytes 589828
  8.9 0.9 %copy-start.5 = (f32[3,21,4,16]{1,3,2,0:T(8,128)S(1)}, f32[3,21,4,16]{1,3,2,0:T(8,128)}, u32[]{:S(2)}) copy-start(f32[3,21,4,16]{1,3,2,0:T(8,128)} %param.9) | copy-start | bytes 48388
  9.7 12.6 %copy-start.1 = (f32[4,16,512]{2,1,0:T(8,128)S(1)}, f32[4,16,512]{2,1,0:T(8,128)}, u32[]{:S(2)}) copy-start(f32[4,16,512]{2,1,0:T(8,128)} %refs_0_.1) | copy-start | bytes 393220
  12.4 9.2 %collective-permute-start.4 = (f32[4,16,512]{2,1,0:T(8,128)S(1)}, f32[4,16,512]{2,1,0:T(8,128)S(1)}, u32[]{:S(2)}, u32[]{:S(2)}) collective-permute-start(f32[4,16,512]{2,1,0:T(8,128)S(1)} %collective-permute-done.one_ref.refs_1_), channel_id=1, source_target_pairs={{0,1},{1,0},{2,3},{3,2},{4,5},{5,4},{6,7},{7,6},{8,9},{9,8},{10,11... | collective-permute-start | bytes 393224 | tf_op jit(solution)/shard_map/ppermute | solution.py:408
  12.4 9.2 %collective-permute-start.5 = (f32[4,16,512]{2,1,0:T(8,128)S(1)}, f32[4,16,512]{2,1,0:T(8,128)S(1)}, u32[]{:S(2)}, u32[]{:S(2)}) collective-permute-start(f32[4,16,512]{2,1,0:T(8,128)S(1)} %collective-permute-done.one_ref.refs_1_), channel_id=1, source_target_pairs={{0,2},{1,3},{4,6},{5,7},{8,10},{9,11},{12,14},{13,15},{18,16},{19,... | collective-permute-start | bytes 393224 | tf_op jit(solution)/shard_map/ppermute | solution.py:408
  16.0 5.5 %collective-permute-start.6 = (f32[88,128]{1,0:T(8,128)S(1)}, f32[88,128]{1,0:T(8,128)S(1)}, u32[]{:S(2)}, u32[]{:S(2)}) collective-permute-start(f32[88,128]{1,0:T(8,128)S(1)} %get-tuple-element.46.weights_ref), channel_id=1, source_target_pairs={{0,16},{1,17},{2,18},{3,19},{4,20},{5,21},{6,22},{7,23},{8,24},{9,... | collective-permute-start | bytes 135176 | tf_op jit(solution)/shard_map/ppermute | solution.py:408
  16.1 6.2 %collective-permute-start.8 = (f32[4,16,512]{2,1,0:T(8,128)S(1)}, f32[4,16,512]{2,1,0:T(8,128)S(1)}, u32[]{:S(2)}, u32[]{:S(2)}) collective-permute-start(f32[4,16,512]{2,1,0:T(8,128)S(1)} %slice.6), channel_id=1, source_target_pairs={{0,8},{1,9},{2,10},{3,11},{4,12},{5,13},{6,14},{7,15},{8,0},{9,1},... | collective-permute-start | bytes 393224 | tf_op jit(solution)/shard_map/ppermute | solution.py:408
  16.7 5.7 %collective-permute-start.9 = (f32[4,16,512]{2,1,0:T(8,128)S(1)}, f32[4,16,512]{2,1,0:T(8,128)S(1)}, u32[]{:S(2)}, u32[]{:S(2)}) collective-permute-start(f32[4,16,512]{2,1,0:T(8,128)S(1)} %slice.7), channel_id=1, source_target_pairs={{0,4},{1,5},{2,6},{3,7},{4,0},{5,1},{6,2},{7,3},{8,12},{9,13},{10,... | collective-permute-start | bytes 393224 | tf_op jit(solution)/shard_map/ppermute | solution.py:408
  21.5 0.8 %collective-permute-start.7 = (f32[4,16,512]{2,1,0:T(8,128)S(1)}, f32[4,16,512]{2,1,0:T(8,128)S(1)}, u32[]{:S(2)}, u32[]{:S(2)}) collective-permute-start(f32[4,16,512]{2,1,0:T(8,128)S(1)} %collective-permute-done.5.refs_0_.refs_2_), channel_id=1, source_target_pairs={{2,3},{3,2},{6,7},{7,6},{10,11},{11,10},{14,15},{15,14},{16,17},{1... | collective-permute-start | bytes 393224 | tf_op jit(solution)/shard_map/ppermute | solution.py:408
  22.4 10.2 %collective-permute-start.10 = (f32[2,32,512]{2,1,0:T(8,128)S(1)}, f32[2,32,512]{2,1,0:T(8,128)S(1)}, u32[]{:S(2)}, u32[]{:S(2)}) collective-permute-start(f32[2,32,512]{2,1,0:T(8,128)S(1)} %get-tuple-element.66), channel_id=1, source_target_pairs={{0,4},{1,5},{2,6},{3,7},{4,0},{5,1},{6,2},{7,3},{8,12},{9,13},{10,... | collective-permute-start | bytes 393224 | tf_op jit(solution)/shard_map/ppermute | solution.py:408
  24.0 8.6 %collective-permute-start.11 = (f32[2,32,512]{2,1,0:T(8,128)S(1)}, f32[2,32,512]{2,1,0:T(8,128)S(1)}, u32[]{:S(2)}, u32[]{:S(2)}) collective-permute-start(f32[2,32,512]{2,1,0:T(8,128)S(1)} %get-tuple-element.67), channel_id=1, source_target_pairs={{0,12},{1,13},{2,14},{3,15},{4,8},{5,9},{6,10},{7,11},{8,4},{9,5},... | collective-permute-start | bytes 393224 | tf_op jit(solution)/shard_map/ppermute | solution.py:408
  28.9 7.6 %copy-start.4 = (f32[4,16,512]{2,1,0:T(8,128)S(1)}, f32[4,16,512]{2,1,0:T(8,128)}, u32[]{:S(2)}) copy-start(f32[4,16,512]{2,1,0:T(8,128)} %recorded_ref.1) | copy-start | bytes 393220
  28.9 7.6 %collective-permute-start.12 = (f32[2,16,512]{2,1,0:T(8,128)S(1)}, f32[2,16,512]{2,1,0:T(8,128)S(1)}, u32[]{:S(2)}, u32[]{:S(2)}) collective-permute-start(f32[2,16,512]{2,1,0:T(8,128)S(1)} %get-tuple-element.70), channel_id=1, source_target_pairs={{0,16},{1,17},{2,18},{3,19},{4,20},{5,21},{6,22},{7,23},{8,24},{9,... | collective-permute-start | bytes 196616 | tf_op jit(solution)/shard_map/ppermute | solution.py:408
  34.9 6.0 %collective-permute-start.13 = (f32[2,16,512]{2,1,0:T(8,128)S(1)}, f32[2,16,512]{2,1,0:T(8,128)S(1)}, u32[]{:S(2)}, u32[]{:S(2)}) collective-permute-start(f32[2,16,512]{2,1,0:T(8,128)S(1)} %get-tuple-element.72), channel_id=1, source_target_pairs={{0,16},{1,17},{2,18},{3,19},{4,20},{5,21},{6,22},{7,23},{8,24},{9,... | collective-permute-start | bytes 196616 | tf_op jit(solution)/shard_map/ppermute | solution.py:408

commit v5 on v3

--- a/solution.py
+++ b/solution.py
@@ -15,7 +15,7 @@
 AXES = ("rcv", "src")
 STEP = 32
 GROUP = 6
-CHUNK = 64
+CHUNK = 128
 
 
 def phases(samples):

time: 41.8 us -> 41.8 us (level)
  transfers between devices with their start and end apart: 14 -> 14, of which waited for: 3 -> 3; matrix products, arithmetic and copies ran while one was open for 0% -> 0% of each run, Pallas kernels for 32% -> 31%
where the time goes in v5:
time: 41.8 us; the launch traced here: 41.5 us
  starting transfers between devices  19.3 us (46%)
  Pallas kernels  13.8 us (33%)
  waiting for transfers between devices  4.62 us (11%)
  local copies, waits for them, and re-layouts  3.73 us (9%)
    ppermute x14, starting transfers between devices, permute(): return lax.ppermute(array, AXES, pairs)  19.3 us
    pallas_call x7, Pallas kernels, call(): pl.pallas_call(kernel, out_shape=shapes, in_specs=[pl.BlockSpec(memory_sp...  13.8 us
    ppermute x14, waiting for transfers between devices, permute(): return lax.ppermute(array, AXES, pairs)  4.62 us
    unnamed x14, local copies, waits for them, and re-layouts  3.72 us
  transfers between devices with their start and end apart: 14, of which 3 were waited for; matrix products, arithmetic and copies ran while one was open for 0% of the time, Pallas kernels for 31%

profile of v5, /device:TPU:0, one launch (start us, length us, event | category | flops | bytes accessed | tf_op | source)
XLA Modules:
  0.0 41.5 jit_solution(8917500048530411990)
XLA Ops:
  0.0 3.0 %collective-permute-start.1 = (f32[8,16,512]{2,1,0:T(8,128)}, f32[8,16,512]{2,1,0:T(8,128)S(1)}, u32[]{:S(2)}, u32[]{:S(2)}) collective-permute-start(f32[8,16,512]{2,1,0:T(8,128)} %right_ref.1), channel_id=1, source_target_pairs={{0,8},{1,9},{2,10},{3,11},{4,12},{5,13},{6,14},{7,15},{8,0},{9,1},... | collective-permute-start | bytes 786440 | tf_op jit(solution)/shard_map/ppermute | solution.py:408
  3.0 1.5 %collective-permute-start.2 = (f32[8,16,512]{2,1,0:T(8,128)}, f32[8,16,512]{2,1,0:T(8,128)S(1)}, u32[]{:S(2)}, u32[]{:S(2)}) collective-permute-start(f32[8,16,512]{2,1,0:T(8,128)} %right_ref.1), channel_id=1, source_target_pairs={{0,4},{1,5},{2,6},{3,7},{4,0},{5,1},{6,2},{7,3},{8,12},{9,13},{10,... | collective-permute-start | bytes 786440 | tf_op jit(solution)/shard_map/ppermute | solution.py:408
  4.5 1.5 %collective-permute-start = (f32[4,16,512]{2,1,0:T(8,128)}, f32[4,16,512]{2,1,0:T(8,128)S(1)}, u32[]{:S(2)}, u32[]{:S(2)}) collective-permute-start(f32[4,16,512]{2,1,0:T(8,128)} %refs_0_.1), channel_id=1, source_target_pairs={{0,2},{1,3},{2,18},{3,19},{4,6},{5,7},{6,22},{7,23},{8,10},{9,11},... | collective-permute-start | bytes 393224 | tf_op jit(solution)/shard_map/ppermute | solution.py:408
  6.0 0.9 %copy-done = f32[4,16,512]{2,1,0:T(8,128)S(1)} copy-done((f32[4,16,512]{2,1,0:T(8,128)S(1)}, f32[4,16,512]{2,1,0:T(8,128)}, u32[]{:S(2)}) %copy-start) | copy-done | bytes 131096
  7.0 0.9 %copy-done.2 = f32[8,16,512]{2,1,0:T(8,128)S(1)} copy-done((f32[8,16,512]{2,1,0:T(8,128)S(1)}, f32[8,16,512]{2,1,0:T(8,128)}, u32[]{:S(2)}) %copy-start.2) | copy-done | bytes 262168
  7.9 0.9 %copy-done.3 = f32[96,512]{1,0:T(8,128)S(1)} copy-done((f32[96,512]{1,0:T(8,128)S(1)}, f32[96,512]{1,0:T(8,128)}, u32[]{:S(2)}) %copy-start.3) | copy-done | bytes 196632
  8.9 0.9 %copy-done.5 = f32[3,21,4,16]{1,3,2,0:T(8,128)S(1)} copy-done((f32[3,21,4,16]{1,3,2,0:T(8,128)S(1)}, f32[3,21,4,16]{1,3,2,0:T(8,128)}, u32[]{:S(2)}) %copy-start.5) | copy-done | bytes 16152
  9.8 1.2 %shard_map.64 = (bf16[512,1024]{1,0:T(8,128)(2,1)S(1)}, bf16[512,1024]{1,0:T(8,128)(2,1)S(1)}, f32[88,128]{1,0:T(8,128)S(1)}, f32[4,16,1536]{2,1,0:T(8,128)S(1)}, f32[8,16,1024]{2,1,0:T(8,128)S(1)}) custom-call(f32[96,512]{1,0:T(8,128)S(1)} %copy-done.3, f32[3,4,16,21]{3,2,1,0:T(8,128)S(1)} %bitcast.1, f32[4,16,512]{2,1,0:T(8,128)S(1)} %copy-done, ...), custom_call_target="tpu_custom_call" | custom-call | tf_op jit(solution)/shard_map/pallas_call | solution.py:384
  11.0 1.4 %collective-permute-done.1.refs_1_ = f32[8,16,512]{2,1,0:T(8,128)S(1)} collective-permute-done((f32[8,16,512]{2,1,0:T(8,128)}, f32[8,16,512]{2,1,0:T(8,128)S(1)}, u32[]{:S(2)}, u32[]{:S(2)}) %collective-permute-start.1) | collective-permute-done | bytes 262176 | tf_op jit(solution)/shard_map/ppermute | solution.py:408
  12.4 3.1 %collective-permute-start.4 = (f32[4,16,512]{2,1,0:T(8,128)S(1)}, f32[4,16,512]{2,1,0:T(8,128)S(1)}, u32[]{:S(2)}, u32[]{:S(2)}) collective-permute-start(f32[4,16,512]{2,1,0:T(8,128)S(1)} %collective-permute-done.one_ref.refs_1_), channel_id=1, source_target_pairs={{0,2},{1,3},{4,6},{5,7},{8,10},{9,11},{12,14},{13,15},{18,16},{19,... | collective-permute-start | bytes 393224 | tf_op jit(solution)/shard_map/ppermute | solution.py:408
  15.8 1.1 %collective-permute-start.8 = (f32[4,16,512]{2,1,0:T(8,128)S(1)}, f32[4,16,512]{2,1,0:T(8,128)S(1)}, u32[]{:S(2)}, u32[]{:S(2)}) collective-permute-start(f32[4,16,512]{2,1,0:T(8,128)S(1)} %slice.6), channel_id=1, source_target_pairs={{0,4},{1,5},{2,6},{3,7},{4,0},{5,1},{6,2},{7,3},{8,12},{9,13},{10,... | collective-permute-start | bytes 393224 | tf_op jit(solution)/shard_map/ppermute | solution.py:408
  16.9 1.3 %collective-permute-start.9 = (f32[4,16,512]{2,1,0:T(8,128)S(1)}, f32[4,16,512]{2,1,0:T(8,128)S(1)}, u32[]{:S(2)}, u32[]{:S(2)}) collective-permute-start(f32[4,16,512]{2,1,0:T(8,128)S(1)} %slice.7), channel_id=1, source_target_pairs={{0,8},{1,9},{2,10},{3,11},{4,12},{5,13},{6,14},{7,15},{8,0},{9,1},... | collective-permute-start | bytes 393224 | tf_op jit(solution)/shard_map/ppermute | solution.py:408
  18.3 1.2 %shard_map.65 = (f32[4,16,1536]{2,1,0:T(8,128)S(1)}, f32[16,16,1024]{2,1,0:T(8,128)S(1)}) custom-call(bf16[512,1024]{1,0:T(8,128)(2,1)S(1)} %get-tuple-element.44.high_ref, bf16[512,1024]{1,0:T(8,128)(2,1)S(1)} %get-tuple-element.45.low_ref, f32[4,16,512]{2,1,0:T(8,128)S(1)} %collective-permute-done.one_ref.refs_1_, ...), custom_call_target="tpu_custom_call" | custom-call | tf_op jit(solution)/shard_map/pallas_call | solution.py:384
  19.4 2.2 %collective-permute-done.6.weights_ref = f32[88,128]{1,0:T(8,128)S(1)} collective-permute-done((f32[88,128]{1,0:T(8,128)S(1)}, f32[88,128]{1,0:T(8,128)S(1)}, u32[]{:S(2)}, u32[]{:S(2)}) %collective-permute-start.6) | collective-permute-done | bytes 45088 | tf_op jit(solution)/shard_map/ppermute | solution.py:408
  21.6 0.7 %collective-permute-start.7 = (f32[4,16,512]{2,1,0:T(8,128)S(1)}, f32[4,16,512]{2,1,0:T(8,128)S(1)}, u32[]{:S(2)}, u32[]{:S(2)}) collective-permute-start(f32[4,16,512]{2,1,0:T(8,128)S(1)} %collective-permute-done.4.refs_0_.refs_2_), channel_id=1, source_target_pairs={{2,3},{3,2},{6,7},{7,6},{10,11},{11,10},{14,15},{15,14},{16,17},{1... | collective-permute-start | bytes 393224 | tf_op jit(solution)/shard_map/ppermute | solution.py:408
  22.3 1.1 %collective-permute-done.9.refs_4_ = f32[4,16,512]{2,1,0:T(8,128)S(1)} collective-permute-done((f32[4,16,512]{2,1,0:T(8,128)S(1)}, f32[4,16,512]{2,1,0:T(8,128)S(1)}, u32[]{:S(2)}, u32[]{:S(2)}) %collective-permute-start.9) | collective-permute-done | bytes 131104 | tf_op jit(solution)/shard_map/ppermute | solution.py:408
  23.4 1.1 %collective-permute-start.10 = (f32[2,32,512]{2,1,0:T(8,128)S(1)}, f32[2,32,512]{2,1,0:T(8,128)S(1)}, u32[]{:S(2)}, u32[]{:S(2)}) collective-permute-start(f32[2,32,512]{2,1,0:T(8,128)S(1)} %get-tuple-element.66), channel_id=1, source_target_pairs={{0,4},{1,5},{2,6},{3,7},{4,0},{5,1},{6,2},{7,3},{8,12},{9,13},{10,... | collective-permute-start | bytes 393224 | tf_op jit(solution)/shard_map/ppermute | solution.py:408
  24.5 0.9 %collective-permute-start.11 = (f32[2,32,512]{2,1,0:T(8,128)S(1)}, f32[2,32,512]{2,1,0:T(8,128)S(1)}, u32[]{:S(2)}, u32[]{:S(2)}) collective-permute-start(f32[2,32,512]{2,1,0:T(8,128)S(1)} %get-tuple-element.67), channel_id=1, source_target_pairs={{0,12},{1,13},{2,14},{3,15},{4,8},{5,9},{6,10},{7,11},{8,4},{9,5},... | collective-permute-start | bytes 393224 | tf_op jit(solution)/shard_map/ppermute | solution.py:408
  25.4 4.0 %shard_map.66 = (f32[2,16,512]{2,1,0:T(8,128)S(1)}, f32[2,16,512]{2,1,0:T(8,128)S(1)}, f32[32,16,1536]{2,1,0:T(8,128)S(1)}) custom-call(s32[21]{0:T(128)S(1)} %copy-done.6, bf16[512,1024]{1,0:T(8,128)(2,1)S(1)} %get-tuple-element.44.high_ref, bf16[512,1024]{1,0:T(8,128)(2,1)S(1)} %get-tuple-element.45.low_ref, ...), custom_call_target="tpu_custom_call" | custom-call | tf_op jit(solution)/shard_map/pallas_call | solution.py:384
  29.4 2.7 %collective-permute-start.12 = (f32[2,16,512]{2,1,0:T(8,128)S(1)}, f32[2,16,512]{2,1,0:T(8,128)S(1)}, u32[]{:S(2)}, u32[]{:S(2)}) collective-permute-start(f32[2,16,512]{2,1,0:T(8,128)S(1)} %get-tuple-element.70), channel_id=1, source_target_pairs={{0,16},{1,17},{2,18},{3,19},{4,20},{5,21},{6,22},{7,23},{8,24},{9,... | collective-permute-start | bytes 196616 | tf_op jit(solution)/shard_map/ppermute | solution.py:408
  32.2 2.3 %shard_map.68 = (f32[2,16,512]{2,1,0:T(8,128)S(1)}, f32[4,32,1536]{2,1,0:T(8,128)S(1)}) custom-call(s32[21]{0:T(128)S(1)} %copy-done.6, bf16[512,1024]{1,0:T(8,128)(2,1)S(1)} %get-tuple-element.44.high_ref, bf16[512,1024]{1,0:T(8,128)(2,1)S(1)} %get-tuple-element.45.low_ref, f32[88,128]{1,0:T(8,128)S(1)} %collective-permute-done.6.weights_ref, ...), custom_call_target="tpu_custom_call" | custom-call | tf_op jit(solution)/shard_map/pallas_call | solution.py:384
  34.5 2.0 %collective-permute-start.13 = (f32[2,16,512]{2,1,0:T(8,128)S(1)}, f32[2,16,512]{2,1,0:T(8,128)S(1)}, u32[]{:S(2)}, u32[]{:S(2)}) collective-permute-start(f32[2,16,512]{2,1,0:T(8,128)S(1)} %get-tuple-element.72), channel_id=1, source_target_pairs={{0,16},{1,17},{2,18},{3,19},{4,20},{5,21},{6,22},{7,23},{8,24},{9,... | collective-permute-start | bytes 196616 | tf_op jit(solution)/shard_map/ppermute | solution.py:408
  36.5 4.4 %shard_map.69.part_ref = f32[4,16,512]{2,1,0:T(8,128)S(1)} custom-call(s32[21]{0:T(128)S(1)} %copy-done.6, bf16[512,1024]{1,0:T(8,128)(2,1)S(1)} %get-tuple-element.44.high_ref, bf16[512,1024]{1,0:T(8,128)(2,1)S(1)} %get-tuple-element.45.low_ref, f32[88,128]{1,0:T(8,128)S(1)} %get-tuple-element.46.weights_ref, ...), custom_call_target="tpu_custom_call" | custom-call | tf_op jit(solution)/shard_map/pallas_call | solution.py:384
  40.9 0.7 %shard_map.70 = f32[4,16,512]{2,1,0:T(8,128)} custom-call(f32[4,16,512]{2,1,0:T(8,128)S(1)} %shard_map.69.part_ref, f32[2,16,512]{2,1,0:T(8,128)S(1)} %collective-permute-done.13.ends_ref), custom_call_target="tpu_custom_call" | custom-call | tf_op jit(solution)/shard_map/pallas_call | solution.py:384
  (27 shorter events, 0.4 us)
Async XLA Ops:
  0.0 25.4 %copy-start.6 = (s32[21]{0:T(128)S(1)}, s32[21]{0:T(128)}, u32[]{:S(2)}) copy-start(s32[21]{0:T(128)} %offsets_from.5) | copy-start | bytes 256
  0.0 12.3 %collective-permute-start.1 = (f32[8,16,512]{2,1,0:T(8,128)}, f32[8,16,512]{2,1,0:T(8,128)S(1)}, u32[]{:S(2)}, u32[]{:S(2)}) collective-permute-start(f32[8,16,512]{2,1,0:T(8,128)} %right_ref.1), channel_id=1, source_target_pairs={{0,8},{1,9},{2,10},{3,11},{4,12},{5,13},{6,14},{7,15},{8,0},{9,1},... | collective-permute-start | bytes 786440 | tf_op jit(solution)/shard_map/ppermute | solution.py:408
  3.0 9.3 %collective-permute-start.2 = (f32[8,16,512]{2,1,0:T(8,128)}, f32[8,16,512]{2,1,0:T(8,128)S(1)}, u32[]{:S(2)}, u32[]{:S(2)}) collective-permute-start(f32[8,16,512]{2,1,0:T(8,128)} %right_ref.1), channel_id=1, source_target_pairs={{0,4},{1,5},{2,6},{3,7},{4,0},{5,1},{6,2},{7,3},{8,12},{9,13},{10,... | collective-permute-start | bytes 786440 | tf_op jit(solution)/shard_map/ppermute | solution.py:408
  4.5 6.4 %collective-permute-start = (f32[4,16,512]{2,1,0:T(8,128)}, f32[4,16,512]{2,1,0:T(8,128)S(1)}, u32[]{:S(2)}, u32[]{:S(2)}) collective-permute-start(f32[4,16,512]{2,1,0:T(8,128)} %refs_0_.1), channel_id=1, source_target_pairs={{0,2},{1,3},{2,18},{3,19},{4,6},{5,7},{6,22},{7,23},{8,10},{9,11},... | collective-permute-start | bytes 393224 | tf_op jit(solution)/shard_map/ppermute | solution.py:408
  6.0 4.9 %collective-permute-start.3 = (f32[4,16,512]{2,1,0:T(8,128)}, f32[4,16,512]{2,1,0:T(8,128)S(1)}, u32[]{:S(2)}, u32[]{:S(2)}) collective-permute-start(f32[4,16,512]{2,1,0:T(8,128)} %refs_0_.1), channel_id=1, source_target_pairs={{0,1},{1,0},{2,3},{3,2},{4,5},{5,4},{6,7},{7,6},{8,9},{9,8},{10,11... | collective-permute-start | bytes 393224 | tf_op jit(solution)/shard_map/ppermute | solution.py:408
  6.0 0.9 %copy-start = (f32[4,16,512]{2,1,0:T(8,128)S(1)}, f32[4,16,512]{2,1,0:T(8,128)}, u32[]{:S(2)}) copy-start(f32[4,16,512]{2,1,0:T(8,128)} %refs_0_.1) | copy-start | bytes 393220
  7.0 0.9 %copy-start.2 = (f32[8,16,512]{2,1,0:T(8,128)S(1)}, f32[8,16,512]{2,1,0:T(8,128)}, u32[]{:S(2)}) copy-start(f32[8,16,512]{2,1,0:T(8,128)} %right_ref.1) | copy-start | bytes 786436
  7.9 0.9 %copy-start.3 = (f32[96,512]{1,0:T(8,128)S(1)}, f32[96,512]{1,0:T(8,128)}, u32[]{:S(2)}) copy-start(f32[96,512]{1,0:T(8,128)} %constant.2.clone.phases_ref) | copy-start | bytes 589828
  8.9 0.9 %copy-start.5 = (f32[3,21,4,16]{1,3,2,0:T(8,128)S(1)}, f32[3,21,4,16]{1,3,2,0:T(8,128)}, u32[]{:S(2)}) copy-start(f32[3,21,4,16]{1,3,2,0:T(8,128)} %param.9) | copy-start | bytes 48388
  9.7 13.6 %copy-start.1 = (f32[4,16,512]{2,1,0:T(8,128)S(1)}, f32[4,16,512]{2,1,0:T(8,128)}, u32[]{:S(2)}) copy-start(f32[4,16,512]{2,1,0:T(8,128)} %refs_0_.1) | copy-start | bytes 393220
  12.4 9.2 %collective-permute-start.4 = (f32[4,16,512]{2,1,0:T(8,128)S(1)}, f32[4,16,512]{2,1,0:T(8,128)S(1)}, u32[]{:S(2)}, u32[]{:S(2)}) collective-permute-start(f32[4,16,512]{2,1,0:T(8,128)S(1)} %collective-permute-done.one_ref.refs_1_), channel_id=1, source_target_pairs={{0,2},{1,3},{4,6},{5,7},{8,10},{9,11},{12,14},{13,15},{18,16},{19,... | collective-permute-start | bytes 393224 | tf_op jit(solution)/shard_map/ppermute | solution.py:408
  15.5 6.1 %collective-permute-start.5 = (f32[4,16,512]{2,1,0:T(8,128)S(1)}, f32[4,16,512]{2,1,0:T(8,128)S(1)}, u32[]{:S(2)}, u32[]{:S(2)}) collective-permute-start(f32[4,16,512]{2,1,0:T(8,128)S(1)} %collective-permute-done.one_ref.refs_1_), channel_id=1, source_target_pairs={{0,1},{1,0},{2,3},{3,2},{4,5},{5,4},{6,7},{7,6},{8,9},{9,8},{10,11... | collective-permute-start | bytes 393224 | tf_op jit(solution)/shard_map/ppermute | solution.py:408
  15.8 5.8 %collective-permute-start.6 = (f32[88,128]{1,0:T(8,128)S(1)}, f32[88,128]{1,0:T(8,128)S(1)}, u32[]{:S(2)}, u32[]{:S(2)}) collective-permute-start(f32[88,128]{1,0:T(8,128)S(1)} %get-tuple-element.46.weights_ref), channel_id=1, source_target_pairs={{0,16},{1,17},{2,18},{3,19},{4,20},{5,21},{6,22},{7,23},{8,24},{9,... | collective-permute-start | bytes 135176 | tf_op jit(solution)/shard_map/ppermute | solution.py:408
  15.8 6.5 %collective-permute-start.8 = (f32[4,16,512]{2,1,0:T(8,128)S(1)}, f32[4,16,512]{2,1,0:T(8,128)S(1)}, u32[]{:S(2)}, u32[]{:S(2)}) collective-permute-start(f32[4,16,512]{2,1,0:T(8,128)S(1)} %slice.6), channel_id=1, source_target_pairs={{0,4},{1,5},{2,6},{3,7},{4,0},{5,1},{6,2},{7,3},{8,12},{9,13},{10,... | collective-permute-start | bytes 393224 | tf_op jit(solution)/shard_map/ppermute | solution.py:408
  16.9 6.4 %collective-permute-start.9 = (f32[4,16,512]{2,1,0:T(8,128)S(1)}, f32[4,16,512]{2,1,0:T(8,128)S(1)}, u32[]{:S(2)}, u32[]{:S(2)}) collective-permute-start(f32[4,16,512]{2,1,0:T(8,128)S(1)} %slice.7), channel_id=1, source_target_pairs={{0,8},{1,9},{2,10},{3,11},{4,12},{5,13},{6,14},{7,15},{8,0},{9,1},... | collective-permute-start | bytes 393224 | tf_op jit(solution)/shard_map/ppermute | solution.py:408
  21.6 1.7 %collective-permute-start.7 = (f32[4,16,512]{2,1,0:T(8,128)S(1)}, f32[4,16,512]{2,1,0:T(8,128)S(1)}, u32[]{:S(2)}, u32[]{:S(2)}) collective-permute-start(f32[4,16,512]{2,1,0:T(8,128)S(1)} %collective-permute-done.4.refs_0_.refs_2_), channel_id=1, source_target_pairs={{2,3},{3,2},{6,7},{7,6},{10,11},{11,10},{14,15},{15,14},{16,17},{1... | collective-permute-start | bytes 393224 | tf_op jit(solution)/shard_map/ppermute | solution.py:408
  23.4 8.8 %collective-permute-start.10 = (f32[2,32,512]{2,1,0:T(8,128)S(1)}, f32[2,32,512]{2,1,0:T(8,128)S(1)}, u32[]{:S(2)}, u32[]{:S(2)}) collective-permute-start(f32[2,32,512]{2,1,0:T(8,128)S(1)} %get-tuple-element.66), channel_id=1, source_target_pairs={{0,4},{1,5},{2,6},{3,7},{4,0},{5,1},{6,2},{7,3},{8,12},{9,13},{10,... | collective-permute-start | bytes 393224 | tf_op jit(solution)/shard_map/ppermute | solution.py:408
  24.5 7.7 %collective-permute-start.11 = (f32[2,32,512]{2,1,0:T(8,128)S(1)}, f32[2,32,512]{2,1,0:T(8,128)S(1)}, u32[]{:S(2)}, u32[]{:S(2)}) collective-permute-start(f32[2,32,512]{2,1,0:T(8,128)S(1)} %get-tuple-element.67), channel_id=1, source_target_pairs={{0,12},{1,13},{2,14},{3,15},{4,8},{5,9},{6,10},{7,11},{8,4},{9,5},... | collective-permute-start | bytes 393224 | tf_op jit(solution)/shard_map/ppermute | solution.py:408
  29.4 7.0 %copy-start.4 = (f32[4,16,512]{2,1,0:T(8,128)S(1)}, f32[4,16,512]{2,1,0:T(8,128)}, u32[]{:S(2)}) copy-start(f32[4,16,512]{2,1,0:T(8,128)} %recorded_ref.1) | copy-start | bytes 393220
  29.4 7.0 %collective-permute-start.12 = (f32[2,16,512]{2,1,0:T(8,128)S(1)}, f32[2,16,512]{2,1,0:T(8,128)S(1)}, u32[]{:S(2)}, u32[]{:S(2)}) collective-permute-start(f32[2,16,512]{2,1,0:T(8,128)S(1)} %get-tuple-element.70), channel_id=1, source_target_pairs={{0,16},{1,17},{2,18},{3,19},{4,20},{5,21},{6,22},{7,23},{8,24},{9,... | collective-permute-start | bytes 196616 | tf_op jit(solution)/shard_map/ppermute | solution.py:408
  34.5 6.4 %collective-permute-start.13 = (f32[2,16,512]{2,1,0:T(8,128)S(1)}, f32[2,16,512]{2,1,0:T(8,128)S(1)}, u32[]{:S(2)}, u32[]{:S(2)}) collective-permute-start(f32[2,16,512]{2,1,0:T(8,128)S(1)} %get-tuple-element.72), channel_id=1, source_target_pairs={{0,16},{1,17},{2,18},{3,19},{4,20},{5,21},{6,22},{7,23},{8,24},{9,... | collective-permute-start | bytes 196616 | tf_op jit(solution)/shard_map/ppermute | solution.py:408
